TPU v7x, 256 devices: a whole 4x4x8 slice. The times are simulated.
256 devices in a mesh: cfg: 2 (over z_lo), seq: 128 (over x, z_hi, y, core).
Axes of the slice: x: 4, y: 4, z: 8 (z_hi: 4, z_lo: 2; z = z_hi * 2 + z_lo), core: 2. Of those that a mesh axis runs over, the one named last changes fastest.
Arguments:
- video_hidden: bfloat16 [2, 8192, 3072], P('cfg', 'seq'), may hold values from -6 to 6
- video_weight: bfloat16 [3072, 1536], replicated, may hold values from -0.109375 to 0.109375
- video_key: bfloat16 [2, 8192, 1536], P('cfg', 'seq'), may hold values from -6 to 6
- video_value: bfloat16 [2, 8192, 1536], P('cfg', 'seq'), may hold values from -6 to 6
- audio_cross_key: bfloat16 [2, 1024, 1536], P('cfg', 'seq'), may hold values from -6 to 6
- audio_cross_value: bfloat16 [2, 1024, 1536], P('cfg', 'seq'), may hold values from -6 to 6
- audio_query: bfloat16 [2, 1024, 1536], P('cfg', 'seq'), may hold values from -6 to 6
- audio_self_query: bfloat16 [2, 1024, 1536], P('cfg', 'seq'), may hold values from -6 to 6
- audio_self_key: bfloat16 [2, 1024, 1536], P('cfg', 'seq'), may hold values from -6 to 6
- audio_self_value: bfloat16 [2, 1024, 1536], P('cfg', 'seq'), may hold values from -6 to 6
- v2a_qgain: float32 [1536], replicated, may hold values from 0.1 to 1.9
- v2a_kgain: float32 [1536], replicated, may hold values from 0.1 to 1.9
- self_qgain: float32 [1536], replicated, may hold values from 0.1 to 1.9
- self_kgain: float32 [1536], replicated, may hold values from 0.1 to 1.9
- a2v_qgain: float32 [1536], replicated, may hold values from 0.1 to 1.9
- a2v_kgain: float32 [1536], replicated, may hold values from 0.1 to 1.9
- video_time: int32 [8192], P('seq'), may hold values from 0 to 2047
- audio_time: int32 [1024], P('seq'), may hold values from 0 to 2047
- branch_keep: int32 [2, 1024], P('cfg', 'seq'), may hold values from 0 to 1, as said below
Outputs:
- video_guided: bfloat16 [8192, 1536], P('seq', 'cfg')
- audio_guided: bfloat16 [1024, 1536], P('seq', 'cfg')
Inputs may be any that keep to these rules, and one draw needn't show every extreme that they name: `branch_keep`: in each branch every audio token whose index is a multiple of 16 is kept.
All inputs are finite; a program needn't handle non-finite values.
Results may differ from a plain program's by a relative error of at most 0.0089.
Values may be sent and summed in bfloat16 or wider, within the bound.
A program may use at most 128 MiB of HBM per device.

v0:
```python
import math

import jax
import jax.numpy as jnp
from jax import lax
from jax.sharding import PartitionSpec as P

HEADS = 12
HEAD_DIM = 128


epsilon = 1e-06
rope_base = 10000.0
guide_scale = 3.0


def rotate_norm(tensor, gain_vec, positions):
    row_count = tensor.shape[0]
    by_head = tensor.astype(jnp.float32).reshape(row_count, HEADS, HEAD_DIM)
    scaled = by_head * lax.rsqrt(jnp.mean(by_head * by_head, axis=-1, keepdims=True) + epsilon)
    scaled = scaled * gain_vec.reshape(HEADS, HEAD_DIM)
    half_dim = HEAD_DIM // 2
    frequencies = rope_base ** (-jnp.arange(half_dim, dtype=jnp.float32) / half_dim)
    angles = positions.astype(jnp.float32)[:, None] * frequencies[None, :]
    cos_table = jnp.cos(angles)[:, None, :]
    sin_table = jnp.sin(angles)[:, None, :]
    lower_half = scaled[..., :half_dim]
    upper_half = scaled[..., half_dim:]
    turned = jnp.concatenate(
        [
            lower_half * cos_table - upper_half * sin_table,
            upper_half * cos_table + lower_half * sin_table,
        ],
        axis=-1,
    )
    return turned.reshape(row_count, HEADS * HEAD_DIM).astype(jnp.bfloat16)


def split_heads(tensor):
    return tensor.reshape(tensor.shape[0], HEADS, HEAD_DIM).transpose(1, 0, 2)


def attend(query_rows, key_rows, value_rows, key_weight):
    row_count = query_rows.shape[0]

    def attend_one_head(head_items):
        head_query, head_key, head_value = head_items
        scores = jnp.dot(head_query, head_key.T, preferred_element_type=jnp.float32) / math.sqrt(
            HEAD_DIM
        )
        weights = jnp.exp(scores) * key_weight[None, :]
        totals = jnp.sum(weights, axis=1, keepdims=True)
        numerator = jnp.dot(
            weights.astype(jnp.bfloat16), head_value, preferred_element_type=jnp.float32
        )
        return numerator / totals

    result = lax.map(
        attend_one_head, (split_heads(query_rows), split_heads(key_rows), split_heads(value_rows))
    )
    return result.transpose(1, 0, 2).reshape(row_count, HEADS * HEAD_DIM)


def partial_attend(query_rows, key_rows, value_rows):
    row_count = query_rows.shape[0]

    def partial_one_head(head_items):
        head_query, head_key, head_value = head_items
        scores = jnp.dot(head_query, head_key.T, preferred_element_type=jnp.float32) / math.sqrt(
            HEAD_DIM
        )
        weights = jnp.exp(scores)
        numerator = jnp.dot(
            weights.astype(jnp.bfloat16), head_value, preferred_element_type=jnp.float32
        )
        return (numerator, jnp.sum(weights, axis=1))

    numerator, totals = lax.map(
        partial_one_head, (split_heads(query_rows), split_heads(key_rows), split_heads(value_rows))
    )
    return (numerator.transpose(1, 0, 2).reshape(row_count, HEADS * HEAD_DIM), totals.T)


def combine_branches(both_parts):
    uncond_f = both_parts[1].astype(jnp.float32)
    return (uncond_f + guide_scale * (both_parts[0].astype(jnp.float32) - uncond_f)).astype(
        jnp.bfloat16
    )


def per_device(
    video_hidden,
    video_weight,
    video_key,
    video_value,
    audio_cross_key,
    audio_cross_value,
    audio_query,
    audio_self_query,
    audio_self_key,
    audio_self_value,
    v2a_qgain,
    v2a_kgain,
    self_qgain,
    self_kgain,
    a2v_qgain,
    a2v_kgain,
    video_time,
    audio_time,
    branch_keep,
):
    audio_count = audio_query.shape[1]
    cross_keys = rotate_norm(audio_cross_key[0], v2a_kgain, audio_time)
    self_keys = rotate_norm(audio_self_key[0], self_kgain, audio_time)
    audio_queries = rotate_norm(audio_query[0], a2v_qgain, audio_time)
    kept_local = branch_keep[0].astype(jnp.bfloat16)
    gathered = (
        lax.all_gather(cross_keys, "seq", axis=0, tiled=True),
        lax.all_gather(audio_cross_value[0], "seq", axis=0, tiled=True),
        lax.all_gather(self_keys, "seq", axis=0, tiled=True),
        lax.all_gather(audio_self_value[0], "seq", axis=0, tiled=True),
        lax.all_gather(audio_queries, "seq", axis=0, tiled=True),
        lax.all_gather(kept_local, "seq", axis=0, tiled=True),
    )
    all_cross_keys, all_cross_values, all_self_keys, all_self_values, all_queries, all_kept = (
        gathered
    )
    kept_float = all_kept.astype(jnp.float32)
    projected = jnp.dot(video_hidden[0], video_weight, preferred_element_type=jnp.float32)
    video_queries = rotate_norm(projected, v2a_qgain, video_time)
    video_keys = rotate_norm(video_key[0], a2v_kgain, video_time)
    numerator, totals = partial_attend(all_queries, video_keys, video_value[0])
    video_part = attend(video_queries, all_cross_keys, all_cross_values, kept_float).astype(
        jnp.bfloat16
    )
    self_queries = rotate_norm(audio_self_query[0], self_qgain, audio_time)
    self_part = attend(self_queries, all_self_keys, all_self_values, kept_float)
    summed_num, summed_tot = lax.psum((numerator, totals), "seq")
    offset = lax.axis_index("seq") * audio_count
    own_num = lax.dynamic_slice_in_dim(summed_num, offset, audio_count, 0)
    own_tot = lax.dynamic_slice_in_dim(summed_tot, offset, audio_count, 0)
    cross_part = (own_num.reshape(audio_count, HEADS, HEAD_DIM) / own_tot[:, :, None]).reshape(
        audio_count, HEADS * HEAD_DIM
    )
    audio_part = (self_part + cross_part).astype(jnp.bfloat16)
    video_both, audio_both = (
        lax.all_to_all(video_part[None], "cfg", split_axis=2, concat_axis=0, tiled=True),
        lax.all_to_all(audio_part[None], "cfg", split_axis=2, concat_axis=0, tiled=True),
    )
    return (combine_branches(video_both), combine_branches(audio_both))


def solution(mesh):
    in_specs = (
        P("cfg", "seq", None),
        P(),
        P("cfg", "seq", None),
        P("cfg", "seq", None),
        P("cfg", "seq", None),
        P("cfg", "seq", None),
        P("cfg", "seq", None),
        P("cfg", "seq", None),
        P("cfg", "seq", None),
        P("cfg", "seq", None),
        P(),
        P(),
        P(),
        P(),
        P(),
        P(),
        P("seq"),
        P("seq"),
        P("cfg", "seq"),
    )
    out_specs = (P("seq", "cfg"), P("seq", "cfg"))
    return jax.shard_map(
        per_device, mesh=mesh, in_specs=in_specs, out_specs=out_specs, check_vma=False
    )
```

profile of v0, /device:TPU:1, one launch (start us, length us, event | category | flops | bytes accessed | tf_op | source)
XLA Modules:
  0.0 1827.9 jit_solution(2772034027332230528)
XLA Ops:
  17.1 12.8 copy.87
  32.7 348.5 %all-reduce = bf16[1024]{0:T(1024)(128)(2,1)S(1)} all-reduce(bf16[1024]{0:T(1024)(128)(2,1)S(1)} %dynamic-update-slice), channel_id=2, replica_groups=mesh['cfg'=2,'seq'=128] {'seq'}, use_global_device_ids=true, to_apply=%add | all-reduce | flops 1024 | bytes 4096
  382.0 5.7 multiply_reduce_fusion.1
  389.5 3.2 copy.101
  392.7 49.2 %while.34 = (s32[]{:T(128)}, f32[12,1024,128]{1,2,0:T(8,128)}, f32[12,1024]{1,0:T(8,128)}, bf16[12,1024,128]{1,2,0:T(8,128)(2,1)S(1)}, bf16[12,64,128]{2,1,0:T(8...) while((s32[]{:T(128)}, f32[12,1024,128]{1,2,0:T(8,128)}, f32[12,1024]{1,0:T(8,128)}, ...), condition=%wide.region_14.15_spmd, body=%wide.region_12.14_spmd.sunk | while | flops 33750016 | bytes 1095769 | solution.py:78
  393.6 1.8 fusion.86
  395.4 1.4 dynamic_update_slice.26
  397.7 1.8 fusion.86
  399.5 1.4 dynamic_update_slice.26
  401.8 1.8 fusion.86
  403.6 1.4 dynamic_update_slice.26
  405.9 1.8 fusion.86
  407.7 1.4 dynamic_update_slice.26
  410.0 1.8 fusion.86
  414.1 1.8 fusion.86
  418.2 1.8 fusion.86
  422.4 1.8 fusion.86
  426.5 1.8 fusion.86
  430.6 1.8 fusion.86
  434.7 1.8 fusion.86
  438.8 1.8 fusion.86
  442.0 3.2 copy.88
  445.2 4.7 copy.89
  449.9 24.7 %while.32 = (s32[]{:T(128)}, bf16[12,64,128]{2,1,0:T(8,128)(2,1)}, bf16[12,64,128]{2,1,0:T(8,128)(2,1)S(1)}, bf16[12,1024,128]{1,2,0:T(8,128)(2,1)S(1)}, f32[102...) while((s32[]{:T(128)}, bf16[12,64,128]{2,1,0:T(8,128)(2,1)}, bf16[12,64,128]{2,1,0:T(8,128)(2,1)S(1)}, ...), condition=%wide.region_4.0_spmd, body=%wide.region_2.4_spmd.sunk | while | flops 33824704 | bytes 842317 | solution.py:58
  450.2 1.8 fusion.78
  452.3 1.8 fusion.78
  454.3 1.8 fusion.78
  456.4 1.8 fusion.78
  458.5 1.8 fusion.78
  460.5 1.8 fusion.78
  462.6 1.8 fusion.78
  464.6 1.8 fusion.78
  466.7 1.8 fusion.78
  468.7 1.8 fusion.78
  470.8 1.8 fusion.78
  472.9 1.8 fusion.78
  476.5 8.8 reduce
  486.3 3.4 all-to-all-start
  489.8 3.2 copy.96
  493.0 4.7 copy.97
  497.8 24.8 %while.33 = (s32[]{:T(128)}, f32[12,8,128]{2,1,0:T(8,128)S(1)}, bf16[12,8,128]{2,1,0:T(8,128)(2,1)}, bf16[12,1024,128]{1,2,0:T(8,128)(2,1)S(1)}, f32[1024]{0:T(1...) while((s32[]{:T(128)}, f32[12,8,128]{2,1,0:T(8,128)S(1)}, bf16[12,8,128]{2,1,0:T(8,128)(2,1)}, ...), condition=%wide.region_9.10_spmd, body=%wide.region_7.9_spmd.sunk | while | flops 4228090 | bytes 569965 | solution.py:58
  522.9 685.3 %psum.15 = f32[1024,12]{0,1:T(8,128)S(1)} all-reduce(f32[1024,12]{0,1:T(8,128)S(1)} %bitcast.214), channel_id=1, replica_groups=mesh['cfg'=2,'seq'=128] {'seq'}, use_global_device_ids=true, to_apply=%region_16.17 | all-reduce | flops 12288 | bytes 98304 | tf_op jit(solution)/shard_map/psum | solution.py:138
  1209.5 586.2 %all-reduce.3.cloned.1.call-done = f32[1024,1536]{0,1:T(8,128)} async-done(((f32[1024,1536]{0,1:T(8,128)}), f32[1024,1536]{0,1:T(8,128)}) %all-reduce.3.cloned.1.call-update) | async-done | bytes 6291472 | tf_op jit(solution)/shard_map/psum | solution.py:138
  1795.7 1.5 fusion.38
  1797.1 6.1 copy.141
  1803.3 8.8 reduce.1
  1813.1 3.2 all-to-all-start.1
  1817.0 2.1 all-to-all-done.1
  (153 shorter events, 72.8 us)
Async XLA Ops:
  7.2 374.8 %copy-start = (bf16[1,64,3072]{2,1,0:T(8,128)(2,1)S(1)}, bf16[1,64,3072]{2,1,0:T(8,128)(2,1)}, u32[]{:S(2)}) copy-start(bf16[1,64,3072]{2,1,0:T(8,128)(2,1)} %param.25) | copy-start | bytes 1179652
  7.2 382.3 %all-gather.13.cloned.1.call-start = ((), (), s32[]{:S(2)}) async-start(), calls=%async_computation.4 | async-start | bytes 3170304 | tf_op jit(solution)/shard_map/all_gather | solution.py:122
  14.0 427.9 %all-gather.9.cloned.1.call-start = ((), (), s32[]{:S(2)}) async-start(), calls=%async_computation.2 | async-start | bytes 3170304 | tf_op jit(solution)/shard_map/all_gather | solution.py:118
  14.8 430.4 %all-gather.15.cloned.1.call-start = ((), (), s32[]{:S(2)}) async-start(), calls=%async_computation.6 | async-start | bytes 3170304 | tf_op jit(solution)/shard_map/all_gather | solution.py:119
  15.5 474.2 %all-gather.11.cloned.1.call-start = ((), (), s32[]{:S(2)}) async-start(), calls=%async_computation.3 | async-start | bytes 3170304 | tf_op jit(solution)/shard_map/all_gather | solution.py:120
  16.3 476.7 %all-gather.17.cloned.1.call-start = ((), (), s32[]{:S(2)}) async-start(), calls=%async_computation.7 | async-start | bytes 3170304 | tf_op jit(solution)/shard_map/all_gather | solution.py:121
  16.9 1778.8 %all-reduce.3.cloned.1.call-start = ((), (), s32[]{:S(2)}) async-start(), calls=%async_computation.5 | async-start | bytes 12582912 | tf_op jit(solution)/shard_map/psum | solution.py:138
  17.0 12.9 copy-start.3
  17.0 13.3 copy-start.8
  17.0 13.3 copy-start.2
  17.0 14.2 copy-start.9
  17.0 14.2 copy-start.10
  382.0 5.9 copy-start.6
  382.0 5.9 copy-start.7
  486.3 721.9 %all-to-all-start = ((bf16[2,2,24576]{2,1,0:T(2,128)(2,1)}), bf16[2,2,24576]{2,1,0:T(2,128)(2,1)S(1)}, u32[]{:S(2)}, u32[]{:S(2)}) async-start(bf16[2,2,24576]{2,1,0:T(2,128)(2,1)} %reshape.277), calls=%async_computation | async-start | bytes 393216 | tf_op jit(solution)/shard_map/all_to_all | solution.py:147
  493.0 4.8 copy-start.5
  497.7 25.1 %copy-start.4 = (f32[12,1024]{1,0:T(8,128)S(1)}, f32[12,1024]{1,0:T(8,128)}, u32[]{:S(2)}) copy-start(f32[12,1024]{1,0:T(8,128)} %get-tuple-element.102) | copy-start | bytes 147460
  1209.2 611.9 %copy-start.1 = (bf16[1,64,3072]{2,1,0:T(8,128)(2,1)S(1)}, bf16[1,64,3072]{2,1,0:T(8,128)(2,1)}, u32[]{:S(2)}) copy-start(bf16[1,64,3072]{2,1,0:T(8,128)(2,1)} %param.25) | copy-start | bytes 1179652
  1813.1 6.0 all-to-all-start.1
Sparse Core Ops, SparseCore 0:
  14.2 81.5 all-gather.12
  99.3 75.1 all-gather.8
  178.1 74.7 all-gather.14
  256.3 75.0 all-gather.10
  334.7 74.9 all-gather.16
  442.1 1353.5 all-reduce.2
where the time goes:
time: 1840 us; the launch traced here: 1830 us
  blocking collectives  1030 us (56%)
  waiting for transfers between devices  590 us (32%)
  matrix products  87.6 us (5%)
  local copies, waits for them, and re-layouts  63.1 us (3%)
  other arithmetic  31.5 us (2%)
    psum x1, blocking collectives, per_device(): summed_num, summed_tot = lax.psum((numerator, totals), 'seq')  685 us
    psum x1, waiting for transfers between devices, per_device(): summed_num, summed_tot = lax.psum((numerator, totals), 'seq')  586 us
    unnamed x1, blocking collectives  349 us
  transfers between devices with their start and end apart: 8, of which 2 were waited for; matrix products, arithmetic and copies ran while one was open for 9% of the time, Pallas kernels for 0%

commit v1 on v0

v1 whole, which is shorter than its diff:
```python
import math

import jax
import jax.numpy as jnp
from jax import lax
from jax.experimental import pallas as pl
from jax.experimental.pallas import tpu as pltpu
from jax.sharding import PartitionSpec as P

HEADS = 12
HEAD_DIM = 128
MESH = pl.DeviceIdType.MESH

epsilon = 1e-06
rope_base = 10000.0
guide_scale = 3.0

GROUP = 3
GW = GROUP * HEAD_DIM
CK, CV, KEEP, SK, SV, AQ = 0, 384, 768, 896, 1280, 1664
SIBLING_LANES = 1664
BLOCK_LANES = 2048
SCORE_SCALE = math.log2(math.e) / math.sqrt(HEAD_DIM)
NT = (((1,), (1,)), ((), ()))


def rope_head(rows, gain, cos, sin):
    mean = jnp.mean(rows * rows, axis=1, keepdims=True)
    scaled = rows * lax.rsqrt(mean + epsilon) * gain
    return scaled * cos + pltpu.roll(scaled, 64, 1) * sin


def weigh(queries, keys, values):
    scores = lax.dot_general(queries, keys, NT, preferred_element_type=jnp.float32)
    weights = jnp.exp2(scores * SCORE_SCALE).astype(jnp.bfloat16)
    return jnp.dot(weights, values, preferred_element_type=jnp.float32)


def head(index):
    return slice(index * HEAD_DIM, (index + 1) * HEAD_DIM)


def kernel(
    hidden,
    weight,
    video_key,
    video_value,
    cross_key,
    cross_value,
    audio_query,
    self_query,
    self_key,
    self_value,
    v2a_qgain,
    v2a_kgain,
    self_qgain,
    self_kgain,
    a2v_qgain,
    a2v_kgain,
    video_cos,
    video_sin,
    audio_cos,
    audio_sin,
    keep,
    video_out,
    audio_out,
    wbuf,
    astage,
    arcv,
    block,
    squery,
    vq_send,
    vk_send,
    vq,
    vk,
    vv,
    partial,
    partials,
    vpart,
    apart,
    vfin,
    afin,
    w_sem,
    za_s,
    za_r,
    zk_s,
    zk_r,
    zv_s,
    zv_r,
    zq_s,
    zq_r,
    x_s,
    x_r,
    y_s,
    y_r,
    fa_s,
    fa_r,
    fb_s,
    fb_r,
    sib_s,
    sib_r,
    sibv_s,
    sibv_r,
    rs_s,
    rs_r,
    vf_s,
    vf_r,
    af_s,
    af_r,
):
    cfg = lax.axis_index("cfg")
    seq = lax.axis_index("seq")
    core = lax.rem(seq, 2)
    y = lax.rem(seq // 2, 4)
    zh = lax.rem(seq // 8, 4)
    x = seq // 32

    def device(cfg_, x_, zh_, y_, core_):
        return (cfg_, ((x_ * 4 + zh_) * 4 + y_) * 2 + core_)

    def plus(value, d):
        return lax.rem(value + d, 4)

    def minus(value, d):
        return lax.rem(value + 4 - d, 4)

    sibling = device(cfg, x, zh, y, 1 - core)

    def remote(src, dst, send, recv, target):
        return pltpu.make_async_remote_copy(
            src_ref=src,
            dst_ref=dst,
            send_sem=send,
            recv_sem=recv,
            device_id=target,
            device_id_type=MESH,
        )

    sends = []

    def start(*args):
        copy = remote(*args)
        copy.start()
        sends.append(copy)

    def arrived(dst, send, recv):
        remote(dst, dst, send, recv, sibling).wait_recv()

    weight_copies = [
        pltpu.make_async_copy(
            weight.at[:, pl.ds(n * 256, 256)], wbuf.at[n], w_sem.at[n]
        )
        for n in range(6)
    ]
    for copy in weight_copies:
        copy.start()

    barrier = pltpu.get_barrier_semaphore()
    peers = [sibling]
    for dx in range(4):
        for dy in range(4):
            if dx or dy:
                peers.append(device(cfg, plus(x, dx), zh, plus(y, dy), core))
    for d in range(4):
        if d:
            peers.append(device(cfg, x, plus(zh, d), y, core))
        peers.append(device(1 - cfg, x, plus(zh, d), y, core))
    for peer in peers:
        pl.semaphore_signal(barrier, inc=1, device_id=peer, device_id_type=MESH)

    acos, asin = audio_cos[...], audio_sin[...]
    mask = keep[...]
    nothing = jnp.zeros((8, HEAD_DIM), jnp.float32)
    for h in range(HEADS):
        at = head(h)

        def rows(ref):
            return ref[0, :, at].astype(jnp.float32)

        pieces = [
            rope_head(rows(audio_query), a2v_qgain[:, at], acos, asin),
            rope_head(rows(self_query), self_qgain[:, at], acos, asin),
            rope_head(rows(cross_key), v2a_kgain[:, at], acos, asin),
            rows(cross_value) * mask,
            rope_head(rows(self_key), self_kgain[:, at], acos, asin),
            rows(self_value) * mask,
            mask,
            nothing,
        ]
        astage[h // GROUP, :, head(h % GROUP)] = jnp.concatenate(pieces, axis=0).astype(
            jnp.bfloat16
        )

    pl.semaphore_wait(barrier, len(peers))

    for d in (1, 3, 2):
        to = plus(zh, d)
        start(
            astage.at[to],
            arcv.at[zh],
            za_s.at[d - 1],
            za_r.at[d - 1],
            device(cfg, x, to, y, core),
        )
    arcv[zh] = astage[zh]

    own_half = pl.multiple_of(core * 256, 256)
    own_rows = pl.multiple_of(core * 256 + zh * 64, 64)
    own_lanes = pl.multiple_of(zh * GW, 128)
    for d in (1, 3, 2):
        to = plus(zh, d)
        start(
            video_value.at[0, :, pl.ds(pl.multiple_of(to * GW, 128), GW)],
            vv.at[pl.ds(own_rows, 64)],
            zv_s.at[d - 1],
            zv_r.at[d - 1],
            device(cfg, x, to, y, core),
        )
    vv[pl.ds(own_rows, 64)] = video_value[0, :, pl.ds(own_lanes, GW)]
    vcos, vsin = video_cos[...], video_sin[...]
    for h in range(HEADS):
        at = head(h)
        vk_send[:, at] = rope_head(
            video_key[0, :, at].astype(jnp.float32), a2v_kgain[:, at], vcos, vsin
        ).astype(jnp.bfloat16)
    for d in (1, 3, 2):
        to = plus(zh, d)
        start(
            vk_send.at[:, pl.ds(pl.multiple_of(to * GW, 128), GW)],
            vk.at[pl.ds(own_rows, 64)],
            zk_s.at[d - 1],
            zk_r.at[d - 1],
            device(cfg, x, to, y, core),
        )
    vk[pl.ds(own_rows, 64)] = vk_send[:, pl.ds(own_lanes, GW)]

    for d in (1, 3, 2):
        arrived(arcv.at[minus(zh, d)], za_s.at[d - 1], za_r.at[d - 1])
    received = [arcv[z].astype(jnp.float32) for z in range(4)]

    def kind(k):
        return jnp.concatenate(
            [one[8 * k : 8 * k + 8] for one in received], axis=0
        ).astype(jnp.bfloat16)

    def base_of(core_, x_, y_):
        return pl.multiple_of(core_ * 512 + (x_ * 4 + y_) * 32, 32)

    own_block = base_of(core, x, y)
    squery[...] = kind(1)
    for k, lane in ((0, AQ), (2, CK), (3, CV), (4, SK), (5, SV)):
        block[pl.ds(own_block, 32), lane : lane + GW] = kind(k)
    block[pl.ds(own_block, 32), KEEP : KEEP + HEAD_DIM] = kind(6)[:, :HEAD_DIM]

    def whole(x_, y_):
        return block.at[pl.ds(base_of(core, x_, y_), 32)]

    def half(x_, y_, which):
        return block.at[pl.ds(pl.multiple_of(base_of(core, x_, y_) + 16 * which, 16), 16)]

    def shared(core_, x_, y_):
        return block.at[pl.ds(base_of(core_, x_, y_), 32), pl.ds(0, SIBLING_LANES)]

    def shared_half(core_, x_, y_, which):
        return block.at[
            pl.ds(pl.multiple_of(base_of(core_, x_, y_) + 16 * which, 16), 16),
            pl.ds(0, SIBLING_LANES),
        ]

    for d in (1, 3, 2):
        start(
            whole(x, y),
            whole(x, y),
            x_s.at[d - 1],
            x_r.at[d - 1],
            device(cfg, plus(x, d), zh, y, core),
        )
        start(
            whole(x, y),
            whole(x, y),
            y_s.at[d - 1],
            y_r.at[d - 1],
            device(cfg, x, zh, plus(y, d), core),
        )
    start(shared(core, x, y), shared(core, x, y), sib_s.at[0], sib_r.at[0], sibling)

    def project(n):
        weight_copies[n].wait()
        product = jnp.dot(hidden[0], wbuf[n], preferred_element_type=jnp.float32)
        for part in range(2):
            at = head(2 * n + part)
            vq_send[:, at] = rope_head(
                product[:, head(part)], v2a_qgain[:, at], vcos, vsin
            ).astype(jnp.bfloat16)

    for n in range(3):
        project(n)

    for d1 in (1, 3, 2):
        sx, sy = minus(x, d1), minus(y, d1)
        arrived(whole(sx, y), x_s.at[d1 - 1], x_r.at[d1 - 1])
        for d2 in (1, 3, 2):
            slot = (d1 - 1) * 3 + d2 - 1
            start(
                half(sx, y, 0),
                half(sx, y, 0),
                fa_s.at[slot],
                fa_r.at[slot],
                device(cfg, x, zh, plus(y, d2), core),
            )
        start(
            shared(core, sx, y), shared(core, sx, y), sib_s.at[d1], sib_r.at[d1], sibling
        )
        arrived(whole(x, sy), y_s.at[d1 - 1], y_r.at[d1 - 1])
        for d2 in (1, 3, 2):
            slot = (d1 - 1) * 3 + d2 - 1
            start(
                half(x, sy, 1),
                half(x, sy, 1),
                fb_s.at[slot],
                fb_r.at[slot],
                device(cfg, plus(x, d2), zh, y, core),
            )
        start(
            shared(core, x, sy),
            shared(core, x, sy),
            sib_s.at[3 + d1],
            sib_r.at[3 + d1],
            sibling,
        )

    for d in (1, 3, 2):
        there = pl.multiple_of(core * 256 + minus(zh, d) * 64, 64)
        arrived(vv.at[pl.ds(there, 64)], zv_s.at[d - 1], zv_r.at[d - 1])
        arrived(vk.at[pl.ds(there, 64)], zk_s.at[d - 1], zk_r.at[d - 1])
    mine = pl.ds(own_half, 256)
    start(vv.at[mine], vv.at[mine], sibv_s.at[0], sibv_r.at[0], sibling)
    start(vk.at[mine], vk.at[mine], sibv_s.at[1], sibv_r.at[1], sibling)

    for n in range(3, 6):
        project(n)
    for d in (1, 3, 2):
        to = plus(zh, d)
        start(
            vq_send.at[:, pl.ds(pl.multiple_of(to * GW, 128), GW)],
            vq.at[pl.ds(pl.multiple_of(zh * 64, 64), 64)],
            zq_s.at[d - 1],
            zq_r.at[d - 1],
            device(cfg, x, to, y, core),
        )
    vq[pl.ds(pl.multiple_of(zh * 64, 64), 64)] = vq_send[:, pl.ds(own_lanes, GW)]

    for d1 in (1, 3, 2):
        for d2 in (1, 3, 2):
            slot = (d1 - 1) * 3 + d2 - 1
            sx, sy = minus(x, d1), minus(y, d2)
            arrived(half(sx, sy, 0), fa_s.at[slot], fa_r.at[slot])
            piece = shared_half(core, sx, sy, 0)
            start(piece, piece, sib_s.at[7 + slot], sib_r.at[7 + slot], sibling)
            sx, sy = minus(x, d2), minus(y, d1)
            arrived(half(sx, sy, 1), fb_s.at[slot], fb_r.at[slot])
            piece = shared_half(core, sx, sy, 1)
            start(piece, piece, sib_s.at[16 + slot], sib_r.at[16 + slot], sibling)

    other = 1 - core
    other_half = pl.ds(pl.multiple_of(other * 256, 256), 256)
    arrived(vv.at[other_half], sibv_s.at[0], sibv_r.at[0])
    arrived(vk.at[other_half], sibv_s.at[1], sibv_r.at[1])
    ones = jnp.ones((512, HEAD_DIM), jnp.bfloat16)
    lane = lax.broadcasted_iota(jnp.int32, (128, HEAD_DIM), 1)
    for dx in (1, 3, 2, 0):
        px = plus(x, dx)
        row = pl.multiple_of(px * 128, 128)
        packed = jnp.zeros((128, HEAD_DIM), jnp.float32)
        for h in range(GROUP):
            queries = block[
                pl.ds(pl.multiple_of(core * 512 + row, 128), 128),
                AQ + h * HEAD_DIM : AQ + (h + 1) * HEAD_DIM,
            ]
            values = jnp.concatenate([vv[:, head(h)], ones], axis=1)
            both = weigh(queries, vk[:, head(h)], values)
            partial[pl.ds(row, 128), head(h)] = both[:, :HEAD_DIM].astype(jnp.bfloat16)
            total = both[:, HEAD_DIM:]
            high = total.astype(jnp.bfloat16).astype(jnp.float32)
            packed = jnp.where(lane // 16 == 2 * h, high, packed)
            packed = jnp.where(lane // 16 == 2 * h + 1, total - high, packed)
        partial[pl.ds(row, 128), GW : GW + HEAD_DIM] = packed.astype(jnp.bfloat16)
        for dy in (1, 3, 2, 0):
            if dx or dy:
                py = plus(y, dy)
                start(
                    partial.at[pl.ds(pl.multiple_of((px * 4 + py) * 32, 32), 32)],
                    partials.at[x * 4 + y],
                    rs_s.at[dx * 4 + dy],
                    rs_r.at[dx * 4 + dy],
                    device(cfg, px, zh, py, core),
                )
    partials[x * 4 + y] = partial[pl.ds(pl.multiple_of((x * 4 + y) * 32, 32), 32)]

    arrived(shared(other, x, y), sib_s.at[0], sib_r.at[0])
    for d1 in (1, 3, 2):
        arrived(shared(other, minus(x, d1), y), sib_s.at[d1], sib_r.at[d1])
        arrived(shared(other, x, minus(y, d1)), sib_s.at[3 + d1], sib_r.at[3 + d1])
    for d1 in (1, 3, 2):
        for d2 in (1, 3, 2):
            slot = (d1 - 1) * 3 + d2 - 1
            arrived(
                shared_half(other, minus(x, d1), minus(y, d2), 0),
                sib_s.at[7 + slot],
                sib_r.at[7 + slot],
            )
            arrived(
                shared_half(other, minus(x, d2), minus(y, d1), 1),
                sib_s.at[16 + slot],
                sib_r.at[16 + slot],
            )
    for d in (1, 3, 2):
        arrived(
            vq.at[pl.ds(pl.multiple_of(minus(zh, d) * 64, 64), 64)],
            zq_s.at[d - 1],
            zq_r.at[d - 1],
        )

    is_final = cfg == zh // 2
    slot_out = cfg * 2 + lax.rem(zh, 2)
    final_cfg = zh // 2
    near_copies = []
    for d in (1, 3, 2, 0):
        z = plus(zh, d)
        row = pl.multiple_of(z * 64, 64)
        for h in range(GROUP):
            values = jnp.concatenate(
                [block[:, CV + h * HEAD_DIM : CV + (h + 1) * HEAD_DIM], block[:, KEEP:SK]],
                axis=1,
            )
            both = weigh(
                vq[pl.ds(row, 64), head(h)],
                block[:, CK + h * HEAD_DIM : CK + (h + 1) * HEAD_DIM],
                values,
            )
            vpart[pl.ds(row, 64), head(h)] = (
                both[:, :HEAD_DIM] / both[:, HEAD_DIM:]
            ).astype(jnp.bfloat16)
        copy = remote(
            vpart.at[pl.ds(row, 64)],
            vfin.at[slot_out],
            vf_s.at[d],
            vf_r.at[slot_out],
            device(final_cfg, x, z, y, core),
        )
        if d:
            copy.start()
            sends.append(copy)
        else:
            pl.when(jnp.logical_not(is_final))(copy.start)
            near_copies.append(copy)

    for h in range(GROUP):
        values = jnp.concatenate(
            [block[:, SV + h * HEAD_DIM : SV + (h + 1) * HEAD_DIM], block[:, KEEP:SK]],
            axis=1,
        )
        both = weigh(
            squery[:, head(h)],
            block[:, SK + h * HEAD_DIM : SK + (h + 1) * HEAD_DIM],
            values,
        )
        apart[:, head(h)] = both[:, :HEAD_DIM] / both[:, HEAD_DIM:]

    for dx in (1, 3, 2, 0):
        for dy in (1, 3, 2, 0):
            if dx or dy:
                arrived(
                    partials.at[minus(x, dx) * 4 + minus(y, dy)],
                    rs_s.at[dx * 4 + dy],
                    rs_r.at[dx * 4 + dy],
                )
    summed = partials[0].astype(jnp.float32)
    for n in range(1, 16):
        summed = summed + partials[n].astype(jnp.float32)
    for h in range(GROUP):
        high = summed[:, GW + 32 * h : GW + 32 * h + 1]
        low = summed[:, GW + 32 * h + 16 : GW + 32 * h + 17]
        part = apart[:, head(h)] + summed[:, head(h)] / (high + low)
        apart[:, head(h)] = part.astype(jnp.bfloat16).astype(jnp.float32)
    for d in (1, 3, 2, 0):
        z = plus(zh, d)
        copy = remote(
            apart.at[pl.ds(pl.multiple_of(z * 8, 8), 8)],
            afin.at[slot_out],
            af_s.at[d],
            af_r.at[slot_out],
            device(final_cfg, x, z, y, core),
        )
        if d:
            copy.start()
            sends.append(copy)
        else:
            pl.when(jnp.logical_not(is_final))(copy.start)
            near_copies.append(copy)

    @pl.when(is_final)
    def _():
        vfin[slot_out] = vpart[pl.ds(pl.multiple_of(zh * 64, 64), 64)]
        afin[slot_out] = apart[pl.ds(pl.multiple_of(zh * 8, 8), 8)]

    def wait_final(fin, send, recv):
        for b in range(2):
            for j in range(2):
                here = jnp.logical_and(cfg == b, zh == 2 * cfg + j)

                @pl.when(jnp.logical_not(here))
                def _():
                    arrived(fin.at[2 * b + j], send.at[0], recv.at[2 * b + j])

    def guide(cond, uncond):
        uncond = uncond.astype(jnp.float32)
        return (uncond + guide_scale * (cond.astype(jnp.float32) - uncond)).astype(
            jnp.bfloat16
        )

    wait_final(vfin, vf_s, vf_r)
    for j in range(2):
        video_out[:, j * GW : (j + 1) * GW] = guide(vfin[j], vfin[2 + j])
    wait_final(afin, af_s, af_r)
    audio_out[...] = jnp.concatenate([guide(afin[j], afin[2 + j]) for j in range(2)], axis=1)

    for copy in sends:
        copy.wait_send()

    @pl.when(jnp.logical_not(is_final))
    def _():
        for copy in near_copies:
            copy.wait_send()


def per_device(
    video_hidden,
    video_weight,
    video_key,
    video_value,
    audio_cross_key,
    audio_cross_value,
    audio_query,
    audio_self_query,
    audio_self_key,
    audio_self_value,
    v2a_qgain,
    v2a_kgain,
    self_qgain,
    self_kgain,
    a2v_qgain,
    a2v_kgain,
    video_time,
    audio_time,
    branch_keep,
):
    half_dim = HEAD_DIM // 2
    frequencies = rope_base ** (-jnp.arange(half_dim, dtype=jnp.float32) / half_dim)
    frequencies = jnp.concatenate([frequencies, frequencies])
    turn = jnp.where(jnp.arange(HEAD_DIM) < half_dim, -1.0, 1.0).astype(jnp.float32)

    def tables(positions):
        angles = positions.astype(jnp.float32)[:, None] * frequencies[None, :]
        return jnp.cos(angles), jnp.sin(angles) * turn

    video_cos, video_sin = tables(video_time)
    audio_cos, audio_sin = tables(audio_time)
    keep = jnp.broadcast_to(branch_keep[0].astype(jnp.float32)[:, None], (8, HEAD_DIM))

    vmem = pl.BlockSpec(memory_space=pltpu.VMEM)
    bf16, f32 = jnp.bfloat16, jnp.float32
    dma = pltpu.SemaphoreType.DMA
    gains = [
        gain.reshape(1, HEADS * HEAD_DIM)
        for gain in (v2a_qgain, v2a_kgain, self_qgain, self_kgain, a2v_qgain, a2v_kgain)
    ]
    return pl.pallas_call(
        kernel,
        out_shape=(
            jax.ShapeDtypeStruct((64, 2 * GW), bf16),
            jax.ShapeDtypeStruct((8, 2 * GW), bf16),
        ),
        in_specs=[vmem, pl.BlockSpec(memory_space=pl.ANY)] + [vmem] * 19,
        out_specs=(vmem, vmem),
        scratch_shapes=[
            pltpu.VMEM((6, 3072, 256), bf16),
            pltpu.VMEM((4, 64, GW), bf16),
            pltpu.VMEM((4, 64, GW), bf16),
            pltpu.VMEM((1024, BLOCK_LANES), bf16),
            pltpu.VMEM((32, GW), bf16),
            pltpu.VMEM((64, 4 * GW), bf16),
            pltpu.VMEM((64, 4 * GW), bf16),
            pltpu.VMEM((256, GW), bf16),
            pltpu.VMEM((512, GW), bf16),
            pltpu.VMEM((512, GW), bf16),
            pltpu.VMEM((512, 512), bf16),
            pltpu.VMEM((16, 32, 512), bf16),
            pltpu.VMEM((256, GW), bf16),
            pltpu.VMEM((32, GW), f32),
            pltpu.VMEM((4, 64, GW), bf16),
            pltpu.VMEM((4, 8, GW), f32),
            dma((6,)),
            dma((3,)),
            dma((3,)),
            dma((3,)),
            dma((3,)),
            dma((3,)),
            dma((3,)),
            dma((3,)),
            dma((3,)),
            dma((3,)),
            dma((3,)),
            dma((3,)),
            dma((3,)),
            dma((9,)),
            dma((9,)),
            dma((9,)),
            dma((9,)),
            dma((25,)),
            dma((25,)),
            dma((2,)),
            dma((2,)),
            dma((16,)),
            dma((16,)),
            dma((4,)),
            dma((4,)),
            dma((4,)),
            dma((4,)),
        ],
        compiler_params=pltpu.CompilerParams(
            collective_id=0, has_side_effects=True, vmem_limit_bytes=48 * 1024 * 1024
        ),
        cost_estimate=pl.CostEstimate(
            flops=2 * 64 * 3072 * 1536 * 3, bytes_accessed=12_000_000, transcendentals=1_700_000
        ),
    )(
        video_hidden,
        video_weight,
        video_key,
        video_value,
        audio_cross_key,
        audio_cross_value,
        audio_query,
        audio_self_query,
        audio_self_key,
        audio_self_value,
        *gains,
        video_cos,
        video_sin,
        audio_cos,
        audio_sin,
        keep,
    )


def solution(mesh):
    in_specs = (
        P("cfg", "seq", None),
        P(),
        P("cfg", "seq", None),
        P("cfg", "seq", None),
        P("cfg", "seq", None),
        P("cfg", "seq", None),
        P("cfg", "seq", None),
        P("cfg", "seq", None),
        P("cfg", "seq", None),
        P("cfg", "seq", None),
        P(),
        P(),
        P(),
        P(),
        P(),
        P(),
        P("seq"),
        P("seq"),
        P("cfg", "seq"),
    )
    out_specs = (P("seq", "cfg"), P("seq", "cfg"))
    return jax.shard_map(
        per_device, mesh=mesh, in_specs=in_specs, out_specs=out_specs, check_vma=False
    )
```

time: 1840 us -> 68.5 us (0.04)
  the two profiles are of different devices: /device:TPU:1 before, /device:TPU:32 now
where the time goes in v1:
time: 68.5 us; the launch traced here: 67.6 us
  Pallas kernels  51.8 us (76%)
  local copies, waits for them, and re-layouts  12.8 us (19%)
  other arithmetic  2.37 us (3%)
    pallas_call x1, Pallas kernels, per_device(): pl.pallas_call(kernel, out_shape=(jax.ShapeDtypeStruct((64, 2 * GW), bf16...  51.8 us
    unnamed x20, local copies, waits for them, and re-layouts  8.51 us
    reshape x6, local copies, waits for them, and re-layouts, per_device(): gain.reshape(1, HEADS * HEAD_DIM)  4.21 us

profile of v1, /device:TPU:32, one launch (start us, length us, event | category | flops | bytes accessed | tf_op | source)
XLA Modules:
  0.0 67.6 jit_solution(1696643084227239322)
XLA Ops:
  0.6 0.7 convert_element_type.16
  1.3 0.7 convert_element_type.17
  1.9 0.7 convert_bitcast_fusion
  2.6 0.1 compare_select_fusion
  2.7 0.1 broadcast_in_dim.12.keep
  2.8 0.7 %reshape.36.v2a_qgain = f32[1,1536]{1,0:T(1,128)S(1)} reshape(f32[1536]{0:T(1024)} %param.29) | data formatting | bytes 12288 | tf_op jit(solution)/shard_map/reshape | solution.py:575
  3.5 0.7 %reshape.37.v2a_kgain = f32[1,1536]{1,0:T(1,128)S(1)} reshape(f32[1536]{0:T(1024)} %param.30) | data formatting | bytes 12288 | tf_op jit(solution)/shard_map/reshape | solution.py:575
  4.2 0.7 %reshape.38.self_qgain = f32[1,1536]{1,0:T(1,128)S(1)} reshape(f32[1536]{0:T(1024)} %param.31) | data formatting | bytes 12288 | tf_op jit(solution)/shard_map/reshape | solution.py:575
  4.9 0.7 %reshape.39.self_kgain = f32[1,1536]{1,0:T(1,128)S(1)} reshape(f32[1536]{0:T(1024)} %param.32) | data formatting | bytes 12288 | tf_op jit(solution)/shard_map/reshape | solution.py:575
  5.6 0.7 %reshape.40.a2v_qgain = f32[1,1536]{1,0:T(1,128)S(1)} reshape(f32[1536]{0:T(1024)} %param.33) | data formatting | bytes 12288 | tf_op jit(solution)/shard_map/reshape | solution.py:575
  6.3 0.7 %reshape.41.a2v_kgain = f32[1,1536]{1,0:T(1,128)S(1)} reshape(f32[1536]{0:T(1024)} %param.34) | data formatting | bytes 12288 | tf_op jit(solution)/shard_map/reshape | solution.py:575
  7.0 0.1 fusion.1
  7.1 0.2 fusion
  7.3 0.0 copy-start
  7.3 1.0 %copy-done = bf16[1,64,3072]{2,1,0:T(8,128)(2,1)S(1)} copy-done((bf16[1,64,3072]{2,1,0:T(8,128)(2,1)S(1)}, bf16[1,64,3072]{2,1,0:T(8,128)(2,1)}, u32[]{:S(2)}) %copy-start) | copy-done | bytes 393240
  8.3 0.0 copy-start.1
  8.3 0.9 %copy-done.1 = bf16[1,64,1536]{2,1,0:T(8,128)(2,1)S(1)} copy-done((bf16[1,64,1536]{2,1,0:T(8,128)(2,1)S(1)}, bf16[1,64,1536]{2,1,0:T(8,128)(2,1)}, u32[]{:S(2)}) %copy-start.1) | copy-done | bytes 196632
  9.2 0.0 copy-start.2
  9.2 0.9 %copy-done.2 = bf16[1,64,1536]{2,1,0:T(8,128)(2,1)S(1)} copy-done((bf16[1,64,1536]{2,1,0:T(8,128)(2,1)S(1)}, bf16[1,64,1536]{2,1,0:T(8,128)(2,1)}, u32[]{:S(2)}) %copy-start.2) | copy-done | bytes 196632
  10.1 0.0 copy-start.3
  10.1 0.7 %copy-done.3 = bf16[1,8,1536]{2,1,0:T(8,128)(2,1)S(1)} copy-done((bf16[1,8,1536]{2,1,0:T(8,128)(2,1)S(1)}, bf16[1,8,1536]{2,1,0:T(8,128)(2,1)}, u32[]{:S(2)}) %copy-start.3) | copy-done | bytes 24600
  10.9 0.0 copy-start.4
  10.9 0.7 %copy-done.4 = bf16[1,8,1536]{2,1,0:T(8,128)(2,1)S(1)} copy-done((bf16[1,8,1536]{2,1,0:T(8,128)(2,1)S(1)}, bf16[1,8,1536]{2,1,0:T(8,128)(2,1)}, u32[]{:S(2)}) %copy-start.4) | copy-done | bytes 24600
  11.6 0.0 copy-start.5
  11.6 0.7 %copy-done.5 = bf16[1,8,1536]{2,1,0:T(8,128)(2,1)S(1)} copy-done((bf16[1,8,1536]{2,1,0:T(8,128)(2,1)S(1)}, bf16[1,8,1536]{2,1,0:T(8,128)(2,1)}, u32[]{:S(2)}) %copy-start.5) | copy-done | bytes 24600
  12.4 0.0 copy-start.6
  12.4 0.7 %copy-done.6 = bf16[1,8,1536]{2,1,0:T(8,128)(2,1)S(1)} copy-done((bf16[1,8,1536]{2,1,0:T(8,128)(2,1)S(1)}, bf16[1,8,1536]{2,1,0:T(8,128)(2,1)}, u32[]{:S(2)}) %copy-start.6) | copy-done | bytes 24600
  13.1 0.0 copy-start.7
  13.1 0.7 %copy-done.7 = bf16[1,8,1536]{2,1,0:T(8,128)(2,1)S(1)} copy-done((bf16[1,8,1536]{2,1,0:T(8,128)(2,1)S(1)}, bf16[1,8,1536]{2,1,0:T(8,128)(2,1)}, u32[]{:S(2)}) %copy-start.7) | copy-done | bytes 24600
  13.8 0.0 copy-start.8
  13.8 0.7 %copy-done.8 = bf16[1,8,1536]{2,1,0:T(8,128)(2,1)S(1)} copy-done((bf16[1,8,1536]{2,1,0:T(8,128)(2,1)S(1)}, bf16[1,8,1536]{2,1,0:T(8,128)(2,1)}, u32[]{:S(2)}) %copy-start.8) | copy-done | bytes 24600
  14.6 51.8 %shard_map.194 = (bf16[64,768]{1,0:T(8,128)(2,1)S(1)}, bf16[8,768]{1,0:T(8,128)(2,1)S(1)}) custom-call(bf16[1,64,3072]{2,1,0:T(8,128)(2,1)S(1)} %copy-done, bf16[3072,1536]{1,0:T(8,128)(2,1)} %weight.1, bf16[1,64,1536]{2,1,0:T(8,128)(2,1)S(1)} %copy-done.1, bf16[1,64,1536]{2,1,0:T(8,128)(2,1)S(1)} %copy-done.2, bf16[1,8,1536]{2,1,0:T(8,128)(2,1)S(1)} %copy-done.3, ...), custom_call_target="tpu_custom_call" | custom-call | flops 1811939328 | bytes 12000000 | tf_op jit(solution)/shard_map/pallas_call | solution.py:578
  66.4 0.6 copy.23
  67.0 0.6 copy.24
  (1 shorter events, 0.0 us)
Async XLA Ops:
  7.3 1.0 %copy-start = (bf16[1,64,3072]{2,1,0:T(8,128)(2,1)S(1)}, bf16[1,64,3072]{2,1,0:T(8,128)(2,1)}, u32[]{:S(2)}) copy-start(bf16[1,64,3072]{2,1,0:T(8,128)(2,1)} %hidden.1) | copy-start | bytes 1179652
  8.3 0.9 %copy-start.1 = (bf16[1,64,1536]{2,1,0:T(8,128)(2,1)S(1)}, bf16[1,64,1536]{2,1,0:T(8,128)(2,1)}, u32[]{:S(2)}) copy-start(bf16[1,64,1536]{2,1,0:T(8,128)(2,1)} %video_key.1) | copy-start | bytes 589828
  9.2 0.9 %copy-start.2 = (bf16[1,64,1536]{2,1,0:T(8,128)(2,1)S(1)}, bf16[1,64,1536]{2,1,0:T(8,128)(2,1)}, u32[]{:S(2)}) copy-start(bf16[1,64,1536]{2,1,0:T(8,128)(2,1)} %video_value.1) | copy-start | bytes 589828
  10.1 0.7 %copy-start.3 = (bf16[1,8,1536]{2,1,0:T(8,128)(2,1)S(1)}, bf16[1,8,1536]{2,1,0:T(8,128)(2,1)}, u32[]{:S(2)}) copy-start(bf16[1,8,1536]{2,1,0:T(8,128)(2,1)} %cross_key.1) | copy-start | bytes 73732
  10.9 0.7 %copy-start.4 = (bf16[1,8,1536]{2,1,0:T(8,128)(2,1)S(1)}, bf16[1,8,1536]{2,1,0:T(8,128)(2,1)}, u32[]{:S(2)}) copy-start(bf16[1,8,1536]{2,1,0:T(8,128)(2,1)} %cross_value.1) | copy-start | bytes 73732
  11.6 0.7 %copy-start.5 = (bf16[1,8,1536]{2,1,0:T(8,128)(2,1)S(1)}, bf16[1,8,1536]{2,1,0:T(8,128)(2,1)}, u32[]{:S(2)}) copy-start(bf16[1,8,1536]{2,1,0:T(8,128)(2,1)} %audio_query.1) | copy-start | bytes 73732
  12.4 0.7 %copy-start.6 = (bf16[1,8,1536]{2,1,0:T(8,128)(2,1)S(1)}, bf16[1,8,1536]{2,1,0:T(8,128)(2,1)}, u32[]{:S(2)}) copy-start(bf16[1,8,1536]{2,1,0:T(8,128)(2,1)} %self_query.1) | copy-start | bytes 73732
  13.1 0.7 %copy-start.7 = (bf16[1,8,1536]{2,1,0:T(8,128)(2,1)S(1)}, bf16[1,8,1536]{2,1,0:T(8,128)(2,1)}, u32[]{:S(2)}) copy-start(bf16[1,8,1536]{2,1,0:T(8,128)(2,1)} %self_key.1) | copy-start | bytes 73732
  13.8 0.7 %copy-start.8 = (bf16[1,8,1536]{2,1,0:T(8,128)(2,1)S(1)}, bf16[1,8,1536]{2,1,0:T(8,128)(2,1)}, u32[]{:S(2)}) copy-start(bf16[1,8,1536]{2,1,0:T(8,128)(2,1)} %self_value.1) | copy-start | bytes 73732

commit v2 on v0

v2 whole, which is shorter than its diff:
```python
import math

import jax
import jax.numpy as jnp
import numpy as np
from jax import lax
from jax.experimental import pallas as pl
from jax.experimental.pallas import tpu as pltpu
from jax.sharding import PartitionSpec as P

HEADS = 12
HEAD_DIM = 128
MESH = pl.DeviceIdType.MESH

epsilon = 1e-06
rope_base = 10000.0
guide_scale = 3.0

GROUP = 3
GW = GROUP * HEAD_DIM
CK, CV, KEEP, KV_LANES = 0, 384, 768, 896
SUM_LANES = GW + HEAD_DIM
SCORE_SCALE = math.log2(math.e) / math.sqrt(HEAD_DIM)
NT = (((1,), (1,)), ((), ()))


def rope_heads(items):
    means = [jnp.mean(rows * rows, axis=1, keepdims=True) for rows, _, _, _ in items]
    scaled = [
        rows * lax.rsqrt(mean + epsilon) * gain
        for mean, (rows, gain, _, _) in zip(means, items)
    ]
    turned = [pltpu.roll(one, 64, 1) for one in scaled]
    return [
        one * cos + other * sin
        for one, other, (_, _, cos, sin) in zip(scaled, turned, items)
    ]


def weigh(queries, keys, values):
    scores = lax.dot_general(queries, keys, NT, preferred_element_type=jnp.float32)
    weights = jnp.exp2(scores * SCORE_SCALE).astype(jnp.bfloat16)
    return jnp.dot(weights, values, preferred_element_type=jnp.float32)


def head(index, base=0):
    return slice(base + index * HEAD_DIM, base + (index + 1) * HEAD_DIM)


TRANSFERS = (
    ("z1", 3),
    ("z2", 3),
    ("zk", 3),
    ("zv", 3),
    ("zq", 3),
    ("g0ax", 3),
    ("g0by", 3),
    ("g0ay", 3),
    ("g0bx", 3),
    ("g1ax", 3),
    ("g1by", 3),
    ("g1ay", 3),
    ("g1bx", 3),
    ("sqx", 3),
    ("sky", 3),
    ("sib", 4),
    ("rs", 16),
    ("ss", 3),
    ("vf", 4),
    ("af", 4),
)
FIRST = {}
for _name, _count in TRANSFERS:
    FIRST[_name] = sum(c for n, c in TRANSFERS if n in FIRST)
SEMAPHORES = sum(c for _, c in TRANSFERS)


def kernel(
    hidden_hbm,
    weight,
    video_key_hbm,
    video_value,
    cross_key_hbm,
    cross_value_hbm,
    audio_query_hbm,
    self_query_hbm,
    self_key_hbm,
    self_value_hbm,
    v2a_qgain_hbm,
    v2a_kgain_hbm,
    self_qgain_hbm,
    self_kgain_hbm,
    a2v_qgain_hbm,
    a2v_kgain_hbm,
    video_time,
    audio_time,
    branch_keep,
    frequency,
    vfin,
    afin,
    hidden_in,
    key_in,
    audio_in,
    gain_in,
    frequency_in,
    video_clock,
    audio_clock,
    keep_in,
    in_sem,
    wbuf,
    w_sem,
    stage1,
    stage2,
    recv1,
    recv2,
    g0,
    g1,
    squery,
    sblock,
    spartial,
    spartials,
    vq_send,
    vk_send,
    vq,
    vk,
    vv,
    partial,
    partials,
    vpart,
    apart,
    send_sem,
    recv_sem,
):
    cfg = lax.axis_index("cfg")
    seq = lax.axis_index("seq")
    core = lax.rem(seq, 2)
    y = lax.rem(seq // 2, 4)
    zh = lax.rem(seq // 8, 4)
    x = seq // 32
    other = 1 - core
    me = core

    def device(cfg_, x_, zh_, y_, core_):
        return (cfg_, ((x_ * 4 + zh_) * 4 + y_) * 2 + core_)

    def plus(value, d):
        return lax.rem(value + d, 4)

    def minus(value, d):
        return lax.rem(value + 4 - d, 4)

    def aligned(value, to):
        return pl.multiple_of(value, to)

    sibling = device(cfg, x, zh, y, other)

    def remote(src, dst, send, recv, target):
        return pltpu.make_async_remote_copy(
            src_ref=src,
            dst_ref=dst,
            send_sem=send_sem.at[send],
            recv_sem=recv_sem.at[recv],
            device_id=target,
            device_id_type=MESH,
        )

    sends = []

    def start(src, dst, name, index, target):
        copy = remote(src, dst, FIRST[name] + index, FIRST[name] + index, target)
        copy.start()
        sends.append(copy)

    def arrived(dst, name, index):
        remote(dst, dst, FIRST[name], FIRST[name] + index, sibling).wait_recv()

    inputs = [
        (audio_time, audio_clock),
        (branch_keep.at[0], keep_in),
        (frequency, frequency_in),
        (audio_query_hbm.at[0], audio_in.at[0]),
        (cross_key_hbm.at[0], audio_in.at[2]),
        (cross_value_hbm.at[0], audio_in.at[3]),
        (a2v_qgain_hbm, gain_in.at[0]),
        (v2a_kgain_hbm, gain_in.at[2]),
        (self_query_hbm.at[0], audio_in.at[1]),
        (self_key_hbm.at[0], audio_in.at[4]),
        (self_value_hbm.at[0], audio_in.at[5]),
        (self_qgain_hbm, gain_in.at[1]),
        (self_kgain_hbm, gain_in.at[3]),
        (video_time, video_clock),
        (video_key_hbm.at[0], key_in),
        (a2v_kgain_hbm, gain_in.at[4]),
        (v2a_qgain_hbm, gain_in.at[5]),
        (hidden_hbm.at[0], hidden_in),
    ]
    input_copies = [
        pltpu.make_async_copy(src, dst, in_sem.at[n])
        for n, (src, dst) in enumerate(inputs)
    ]
    for copy in input_copies:
        copy.start()

    barrier = pltpu.get_barrier_semaphore()
    peers = [sibling]
    for dx in range(4):
        for dy in range(4):
            if dx or dy:
                peers.append(device(cfg, plus(x, dx), zh, plus(y, dy), core))
    for d in range(4):
        if d:
            peers.append(device(cfg, x, plus(zh, d), y, core))
        peers.append(device(1 - cfg, x, plus(zh, d), y, core))
    for peer in peers:
        pl.semaphore_signal(barrier, inc=1, device_id=peer, device_id_type=MESH)

    weight_copies = [
        pltpu.make_async_copy(
            weight.at[:, pl.ds(n * 256, 256)], wbuf.at[n], w_sem.at[n]
        )
        for n in range(6)
    ]
    for copy in weight_copies:
        copy.start()

    def spread(scalars, count):
        row = lax.broadcasted_iota(jnp.int32, (8, HEAD_DIM), 0)
        tiles = []
        for first in range(0, count, 8):
            tile = jnp.zeros((8, HEAD_DIM), jnp.int32)
            for r in range(8):
                tile = jnp.where(row == r, scalars[first + r], tile)
            tiles.append(tile)
        return jnp.concatenate(tiles, axis=0).astype(jnp.float32)

    def tables(scalars, count):
        angles = spread(scalars, count) * frequency_in[...]
        lanes = lax.broadcasted_iota(jnp.int32, (count, HEAD_DIM), 1)
        sin = jnp.sin(angles)
        return jnp.cos(angles), jnp.where(lanes < HEAD_DIM // 2, -sin, sin)

    def gain(which, h):
        return gain_in[which, head(h)].reshape(1, HEAD_DIM)

    def audio_rows(which, h):
        return audio_in[which, :, head(h)].astype(jnp.float32)

    for copy in input_copies[:8]:
        copy.wait()
    acos, asin = tables(audio_clock, 8)
    mask = spread(keep_in, 8)
    nothing = jnp.zeros((8, HEAD_DIM), jnp.float32)
    ropes = rope_heads(
        [(audio_rows(0, h), gain(0, h), acos, asin) for h in range(HEADS)]
        + [(audio_rows(2, h), gain(2, h), acos, asin) for h in range(HEADS)]
    )
    values = [audio_rows(3, h) * mask for h in range(HEADS)]
    for h in range(HEADS):
        pieces = [ropes[h], ropes[HEADS + h], values[h], mask]
        stage1[h // GROUP, :, head(h % GROUP)] = jnp.concatenate(pieces, axis=0).astype(
            jnp.bfloat16
        )

    pl.semaphore_wait(barrier, len(peers))

    for d in (1, 3, 2):
        to = plus(zh, d)
        start(stage1.at[to], recv1.at[zh], "z1", d - 1, device(cfg, x, to, y, core))
    recv1[zh] = stage1[zh]

    for copy in input_copies[8:13]:
        copy.wait()
    ropes = rope_heads(
        [(audio_rows(1, h), gain(1, h), acos, asin) for h in range(HEADS)]
        + [(audio_rows(4, h), gain(3, h), acos, asin) for h in range(HEADS)]
    )
    values = [audio_rows(5, h) * mask for h in range(HEADS)]
    for h in range(HEADS):
        pieces = [ropes[h], ropes[HEADS + h], values[h], nothing]
        stage2[h // GROUP, :, head(h % GROUP)] = jnp.concatenate(pieces, axis=0).astype(
            jnp.bfloat16
        )
    for d in (1, 3, 2):
        to = plus(zh, d)
        start(stage2.at[to], recv2.at[zh], "z2", d - 1, device(cfg, x, to, y, core))
    recv2[zh] = stage2[zh]

    for copy in input_copies[13:16]:
        copy.wait()
    vcos, vsin = tables(video_clock, 64)
    for first in range(0, HEADS, 4):
        ropes = rope_heads(
            [
                (key_in[:, head(h)].astype(jnp.float32), gain(4, h), vcos, vsin)
                for h in range(first, first + 4)
            ]
        )
        vk_send[:, first * HEAD_DIM : (first + 4) * HEAD_DIM] = jnp.concatenate(
            ropes, axis=1
        ).astype(jnp.bfloat16)

    for copy in input_copies[16:] + weight_copies:
        copy.wait()

    def project(chunks):
        products = [
            jnp.dot(hidden_in[...], wbuf[n], preferred_element_type=jnp.float32)
            for n in chunks
        ]
        ropes = rope_heads(
            [
                (products[i][:, head(part)], gain(5, 2 * n + part), vcos, vsin)
                for i, n in enumerate(chunks)
                for part in range(2)
            ]
        )
        for i, n in enumerate(chunks):
            vq_send[:, 256 * n : 256 * n + 256] = jnp.concatenate(
                ropes[2 * i : 2 * i + 2], axis=1
            ).astype(jnp.bfloat16)

    for chunks in ((0, 1), (2, 3), (4, 5)):
        project(chunks)

    own_rows = aligned(core * 256 + zh * 64, 64)
    own_lanes = aligned(zh * GW, 128)
    for d in (1, 3, 2):
        to = plus(zh, d)
        lanes = pl.ds(aligned(to * GW, 128), GW)
        target = device(cfg, x, to, y, core)
        start(vk_send.at[:, lanes], vk.at[pl.ds(own_rows, 64)], "zk", d - 1, target)
        start(video_value.at[0, :, lanes], vv.at[pl.ds(own_rows, 64)], "zv", d - 1, target)
    own_value = pltpu.make_async_copy(
        video_value.at[0, :, pl.ds(own_lanes, GW)], vv.at[pl.ds(own_rows, 64)], in_sem.at[18]
    )
    own_value.start()
    vk[pl.ds(own_rows, 64)] = vk_send[:, pl.ds(own_lanes, GW)]

    vq_rows = pl.ds(aligned(zh * 64, 64), 64)
    for d in (1, 3, 2):
        to = plus(zh, d)
        start(
            vq_send.at[:, pl.ds(aligned(to * GW, 128), GW)],
            vq.at[vq_rows],
            "zq",
            d - 1,
            device(cfg, x, to, y, core),
        )
    vq[vq_rows] = vq_send[:, pl.ds(own_lanes, GW)]

    def base_a(core_, x_, y_):
        return core_ * 512 + (y_ * 4 + x_) * 16

    def base_b(core_, x_, y_):
        return core_ * 512 + 256 + (x_ * 4 + y_) * 16

    def own(base, count):
        return pl.ds(aligned(base, 16), count)

    def rows_of(recv):
        received = [recv[z].astype(jnp.float32) for z in range(4)]

        def rows(k):
            return jnp.concatenate(
                [one[8 * k : 8 * k + 8] for one in received], axis=0
            ).astype(jnp.bfloat16)

        return [rows(k) for k in range(4)]

    def place(ref, core, lane, rows):
        lanes = slice(lane, lane + rows.shape[1])
        ref[own(base_a(core, x, y), 16), lanes] = rows[:16]
        ref[own(base_b(core, x, y), 16), lanes] = rows[16:]

    def first_phase(ref, name, core):
        mine_a = ref.at[own(base_a(core, x, y), 16)]
        mine_b = ref.at[own(base_b(core, x, y), 16)]
        for d in (1, 3, 2):
            start(
                mine_a, mine_a, name + "ax", d - 1, device(cfg, plus(x, d), zh, y, me)
            )
            start(
                mine_b, mine_b, name + "by", d - 1, device(cfg, x, zh, plus(y, d), me)
            )

    def second_phase(ref, name, core):
        for d in (1, 3, 2):
            arrived(
                ref.at[own(base_a(core, minus(x, d), y), 16)], name + "ax", d - 1
            )
            arrived(
                ref.at[own(base_b(core, x, minus(y, d)), 16)], name + "by", d - 1
            )
        row_a = ref.at[own(base_a(core, 0, y), 64)]
        row_b = ref.at[own(base_b(core, x, 0), 64)]
        for d in (1, 3, 2):
            start(
                row_a, row_a, name + "ay", d - 1, device(cfg, x, zh, plus(y, d), me)
            )
            start(
                row_b, row_b, name + "bx", d - 1, device(cfg, plus(x, d), zh, y, me)
            )

    def gathered(ref, name, core):
        for d in (1, 3, 2):
            arrived(ref.at[own(base_a(core, 0, minus(y, d)), 64)], name + "ay", d - 1)
            arrived(ref.at[own(base_b(core, minus(x, d), 0), 64)], name + "bx", d - 1)

    for d in (1, 3, 2):
        arrived(recv1.at[minus(zh, d)], "z1", d - 1)
    queries, keys, values, kept = rows_of(recv1)
    kept = kept[:, :HEAD_DIM]
    place(g0, 0, 0, queries)
    first_phase(g0, "g0", 0)
    place(g1, core, CK, keys)
    place(g1, core, CV, values)
    place(g1, core, KEEP, kept)
    first_phase(g1, "g1", core)

    for d in (1, 3, 2):
        arrived(recv2.at[minus(zh, d)], "z2", d - 1)
    queries, keys, values, _ = rows_of(recv2)
    srows = pl.ds(aligned(x * 32, 32), 32)
    squery[srows] = queries
    brows = pl.ds(aligned(core * 128 + y * 32, 32), 32)
    sblock[brows, CK : CK + GW] = keys
    sblock[brows, CV : CV + GW] = values
    sblock[brows, KEEP : KEEP + HEAD_DIM] = kept
    for d in (1, 3, 2):
        start(
            squery.at[srows], squery.at[srows], "sqx", d - 1, device(cfg, plus(x, d), zh, y, core)
        )
        start(
            sblock.at[brows], sblock.at[brows], "sky", d - 1, device(cfg, x, zh, plus(y, d), core)
        )

    second_phase(g0, "g0", 0)
    second_phase(g1, "g1", core)

    for d in (1, 3, 2):
        arrived(sblock.at[pl.ds(aligned(core * 128 + minus(y, d) * 32, 32), 32)], "sky", d - 1)
    mine = sblock.at[pl.ds(aligned(core * 128, 128), 128)]
    start(mine, mine, "sib", 3, sibling)
    for d in (1, 3, 2):
        arrived(squery.at[pl.ds(aligned(minus(x, d) * 32, 32), 32)], "sqx", d - 1)
    arrived(sblock.at[pl.ds(aligned(other * 128, 128), 128)], "sib", 3)

    def pack(put, results):
        lane = lax.broadcasted_iota(jnp.int32, results[0].shape, 1)
        lane = lane[:, :HEAD_DIM] // 16
        totals = jnp.zeros(lane.shape, jnp.float32)
        for h, both in enumerate(results):
            put(head(h), both[:, :HEAD_DIM].astype(jnp.bfloat16))
            total = both[:, HEAD_DIM:]
            high = total.astype(jnp.bfloat16).astype(jnp.float32)
            totals = jnp.where(lane == 2 * h, high, totals)
            totals = jnp.where(lane == 2 * h + 1, total - high, totals)
        put(slice(GW, SUM_LANES), totals.astype(jnp.bfloat16))

    def put_self(lanes, rows):
        spartial[:, lanes] = rows

    pack(
        put_self,
        [
            weigh(
                squery[:, head(h)],
                sblock[:, head(h, CK)],
                jnp.concatenate([sblock[:, head(h, CV)], sblock[:, KEEP:KV_LANES]], axis=1),
            )
            for h in range(GROUP)
        ],
    )
    for d in (1, 3, 2):
        px = plus(x, d)
        start(
            spartial.at[pl.ds(aligned(px * 32, 32), 32)],
            spartials.at[x],
            "ss",
            d - 1,
            device(cfg, px, zh, y, core),
        )
    spartials[x] = spartial[srows]

    own_value.wait()
    for d in (1, 3, 2):
        there = pl.ds(aligned(core * 256 + minus(zh, d) * 64, 64), 64)
        arrived(vk.at[there], "zk", d - 1)
        arrived(vv.at[there], "zv", d - 1)
    mine = pl.ds(aligned(core * 256, 256), 256)
    theirs = pl.ds(aligned(other * 256, 256), 256)
    start(vk.at[mine], vk.at[mine], "sib", 0, sibling)
    start(vv.at[mine], vv.at[mine], "sib", 1, sibling)

    gathered(g0, "g0", 0)

    arrived(vk.at[theirs], "sib", 0)
    arrived(vv.at[theirs], "sib", 1)
    ones = jnp.ones((512, HEAD_DIM), jnp.bfloat16)
    for pair in ((1, 3), (2, 0)):
        spots = []
        for dx in pair:
            px = plus(x, dx)
            for which in range(2):
                for py in range(4):
                    spots.append((px, py, which))

        def put(lanes, rows):
            for n, (px, py, which) in enumerate(spots):
                row = aligned((px * 4 + py) * 32 + 16 * which, 16)
                partial[pl.ds(row, 16), lanes] = rows[16 * n : 16 * n + 16]

        results = []
        for h in range(GROUP):
            queries = []
            for dx in pair:
                px = plus(x, dx)
                for py in range(4):
                    queries.append(g0[own(base_a(0, px, py), 16), head(h)])
                queries.append(g0[own(base_b(0, px, 0), 64), head(h)])
            results.append(
                weigh(
                    jnp.concatenate(queries, axis=0),
                    vk[:, head(h)],
                    jnp.concatenate([vv[:, head(h)], ones], axis=1),
                )
            )
        pack(put, results)
        for dx in pair:
            px = plus(x, dx)
            for dy in (1, 3, 2, 0):
                if dx or dy:
                    py = plus(y, dy)
                    start(
                        partial.at[pl.ds(aligned((px * 4 + py) * 32, 32), 32)],
                        partials.at[x * 4 + y],
                        "rs",
                        dx * 4 + dy,
                        device(cfg, px, zh, py, core),
                    )
    partials[x * 4 + y] = partial[pl.ds(aligned((x * 4 + y) * 32, 32), 32)]

    gathered(g1, "g1", core)
    mine = g1.at[pl.ds(aligned(core * 512, 512), 512)]
    start(mine, mine, "sib", 2, sibling)
    arrived(g1.at[pl.ds(aligned(other * 512, 512), 512)], "sib", 2)
    for d in (1, 3, 2):
        arrived(vq.at[pl.ds(aligned(minus(zh, d) * 64, 64), 64)], "zq", d - 1)

    is_final = cfg == zh // 2
    slot_out = cfg * 2 + lax.rem(zh, 2)
    final_cfg = zh // 2
    near_copies = []

    def final(src, dst, name, d):
        copy = remote(
            src,
            dst,
            FIRST[name] + d,
            FIRST[name] + slot_out,
            device(final_cfg, x, plus(zh, d), y, core),
        )
        if d:
            copy.start()
            sends.append(copy)
        else:
            pl.when(jnp.logical_not(is_final))(copy.start)
            near_copies.append(copy)

    for pair in ((1, 3), (2, 0)):
        rows = [aligned(plus(zh, d) * 64, 64) for d in pair]
        for h in range(GROUP):
            both = weigh(
                jnp.concatenate([vq[pl.ds(row, 64), head(h)] for row in rows], axis=0),
                g1[:, head(h, CK)],
                jnp.concatenate([g1[:, head(h, CV)], g1[:, KEEP:KV_LANES]], axis=1),
            )
            done = (both[:, :HEAD_DIM] / both[:, HEAD_DIM:]).astype(jnp.bfloat16)
            for n, row in enumerate(rows):
                vpart[pl.ds(row, 64), head(h)] = done[64 * n : 64 * n + 64]
        for d, row in zip(pair, rows):
            final(vpart.at[pl.ds(row, 64)], vfin.at[slot_out], "vf", d)

    for dx in (1, 3, 2, 0):
        for dy in (1, 3, 2, 0):
            if dx or dy:
                arrived(
                    partials.at[minus(x, dx) * 4 + minus(y, dy)], "rs", dx * 4 + dy
                )
    for d in (1, 3, 2):
        arrived(spartials.at[minus(x, d)], "ss", d - 1)

    def quotients(ref, count):
        summed = ref[0].astype(jnp.float32)
        for n in range(1, count):
            summed = summed + ref[n].astype(jnp.float32)
        result = []
        for h in range(GROUP):
            high = summed[:, GW + 32 * h : GW + 32 * h + 1]
            low = summed[:, GW + 32 * h + 16 : GW + 32 * h + 17]
            result.append(summed[:, head(h)] / (high + low))
        return jnp.concatenate(result, axis=1)

    part = quotients(spartials, 4) + quotients(partials, 16)
    apart[...] = part.astype(jnp.bfloat16).astype(jnp.float32)
    for d in (1, 3, 2, 0):
        row = aligned(plus(zh, d) * 8, 8)
        final(apart.at[pl.ds(row, 8)], afin.at[slot_out], "af", d)

    @pl.when(is_final)
    def _():
        own_copies = [
            pltpu.make_async_copy(
                vpart.at[pl.ds(aligned(zh * 64, 64), 64)], vfin.at[slot_out], in_sem.at[19]
            ),
            pltpu.make_async_copy(
                apart.at[pl.ds(aligned(zh * 8, 8), 8)], afin.at[slot_out], in_sem.at[20]
            ),
        ]
        for copy in own_copies:
            copy.start()
        for copy in own_copies:
            copy.wait()

    for fin, name in ((vfin, "vf"), (afin, "af")):
        for b in range(2):
            for j in range(2):
                here = jnp.logical_and(cfg == b, zh == 2 * cfg + j)

                @pl.when(jnp.logical_not(here))
                def _():
                    arrived(fin.at[2 * b + j], name, 2 * b + j)

    for copy in sends:
        copy.wait_send()

    @pl.when(jnp.logical_not(is_final))
    def _():
        for copy in near_copies:
            copy.wait_send()


def guide_kernel(video, audio, video_out, audio_out):
    def guide(cond, uncond):
        uncond = uncond.astype(jnp.float32)
        return (uncond + guide_scale * (cond.astype(jnp.float32) - uncond)).astype(
            jnp.bfloat16
        )

    for j in range(2):
        video_out[:, j * GW : (j + 1) * GW] = guide(video[j], video[2 + j])
    audio_out[...] = jnp.concatenate(
        [guide(audio[j], audio[2 + j]) for j in range(2)], axis=1
    )


def per_device(
    video_hidden,
    video_weight,
    video_key,
    video_value,
    audio_cross_key,
    audio_cross_value,
    audio_query,
    audio_self_query,
    audio_self_key,
    audio_self_value,
    v2a_qgain,
    v2a_kgain,
    self_qgain,
    self_kgain,
    a2v_qgain,
    a2v_kgain,
    video_time,
    audio_time,
    branch_keep,
):
    half_dim = HEAD_DIM // 2
    steps = np.arange(half_dim, dtype=np.float32) / np.float32(half_dim)
    frequencies = np.float32(rope_base) ** -steps
    frequencies = np.concatenate([frequencies, frequencies]).reshape(1, HEAD_DIM)

    vmem = pl.BlockSpec(memory_space=pltpu.VMEM)
    bf16, f32 = jnp.bfloat16, jnp.float32
    dma = pltpu.SemaphoreType.DMA
    hbm = pl.BlockSpec(memory_space=pltpu.HBM)
    parts = pl.pallas_call(
        kernel,
        out_shape=(
            jax.ShapeDtypeStruct((4, 64, GW), bf16),
            jax.ShapeDtypeStruct((4, 8, GW), f32),
        ),
        in_specs=[hbm] * 20,
        out_specs=(hbm, hbm),
        scratch_shapes=[
            pltpu.VMEM((64, 3072), bf16),
            pltpu.VMEM((64, 4 * GW), bf16),
            pltpu.VMEM((6, 8, 4 * GW), bf16),
            pltpu.VMEM((6, 4 * GW), f32),
            pltpu.VMEM((1, HEAD_DIM), f32),
            pltpu.SMEM((64,), jnp.int32),
            pltpu.SMEM((8,), jnp.int32),
            pltpu.SMEM((8,), jnp.int32),
            dma((21,)),
            pltpu.VMEM((6, 3072, 256), bf16),
            dma((6,)),
            pltpu.VMEM((4, 32, GW), bf16),
            pltpu.VMEM((4, 32, GW), bf16),
            pltpu.VMEM((4, 32, GW), bf16),
            pltpu.VMEM((4, 32, GW), bf16),
            pltpu.VMEM((512, GW), bf16),
            pltpu.VMEM((1024, KV_LANES), bf16),
            pltpu.VMEM((128, GW), bf16),
            pltpu.VMEM((256, KV_LANES), bf16),
            pltpu.VMEM((128, SUM_LANES), bf16),
            pltpu.VMEM((4, 32, SUM_LANES), bf16),
            pltpu.VMEM((64, 4 * GW), bf16),
            pltpu.VMEM((64, 4 * GW), bf16),
            pltpu.VMEM((256, GW), bf16),
            pltpu.VMEM((512, GW), bf16),
            pltpu.VMEM((512, GW), bf16),
            pltpu.VMEM((512, 512), bf16),
            pltpu.VMEM((16, 32, 512), bf16),
            pltpu.VMEM((256, GW), bf16),
            pltpu.VMEM((32, GW), f32),
            dma((SEMAPHORES,)),
            dma((SEMAPHORES,)),
        ],
        compiler_params=pltpu.CompilerParams(
            collective_id=0, has_side_effects=True, vmem_limit_bytes=64 * 1024 * 1024
        ),
        cost_estimate=pl.CostEstimate(
            flops=2 * 64 * 3072 * 1536 * 3, bytes_accessed=12_000_000, transcendentals=1_700_000
        ),
    )(
        video_hidden,
        video_weight,
        video_key,
        video_value,
        audio_cross_key,
        audio_cross_value,
        audio_query,
        audio_self_query,
        audio_self_key,
        audio_self_value,
        v2a_qgain,
        v2a_kgain,
        self_qgain,
        self_kgain,
        a2v_qgain,
        a2v_kgain,
        video_time,
        audio_time,
        branch_keep,
        frequencies,
    )
    return pl.pallas_call(
        guide_kernel,
        out_shape=(
            jax.ShapeDtypeStruct((64, 2 * GW), bf16),
            jax.ShapeDtypeStruct((8, 2 * GW), bf16),
        ),
        in_specs=[vmem, vmem],
        out_specs=(vmem, vmem),
    )(*parts)


def solution(mesh):
    in_specs = (
        P("cfg", "seq", None),
        P(),
        P("cfg", "seq", None),
        P("cfg", "seq", None),
        P("cfg", "seq", None),
        P("cfg", "seq", None),
        P("cfg", "seq", None),
        P("cfg", "seq", None),
        P("cfg", "seq", None),
        P("cfg", "seq", None),
        P(),
        P(),
        P(),
        P(),
        P(),
        P(),
        P("seq"),
        P("seq"),
        P("cfg", "seq"),
    )
    out_specs = (P("seq", "cfg"), P("seq", "cfg"))
    return jax.shard_map(
        per_device, mesh=mesh, in_specs=in_specs, out_specs=out_specs, check_vma=False
    )
```

time: 1840 us -> 47 us (0.03)
  blocking collectives: 1030 us -> 0 us
  waiting for transfers between devices: 590 us -> 0 us
  matrix products: 87.6 us -> 0 us
  local copies, waits for them, and re-layouts: 63.1 us -> 0 us
  Pallas kernels: 0 us -> 46.3 us
  other arithmetic: 31.5 us -> 0 us
    psum x1 -> x0, blocking collectives: 685 us -> none  [per_device(): summed_num, summed_tot = lax.psum((numerator, totals), 'seq')]
    psum x1 -> x0, waiting for transfers between devices: 586 us -> none  [per_device(): summed_num, summed_tot = lax.psum((numerator, totals), 'seq')]
    unnamed x1 -> x0, blocking collectives: 349 us -> none
    dot_general x73 -> x0, matrix products: 87.6 us -> none  [the longest x24 34.6 us: attend_one_head(): jnp.dot(weights.astype(jnp.bfloat16), head_value, preferred_element_type=...]
    pallas_call x0 -> x2, Pallas kernels: none -> 46.3 us  [the longest x1 44.7 us: per_device(): pl.pallas_call(kernel, out_shape=(jax.ShapeDtypeStruct((4, 64, GW), bf16)...]
    all_gather x5 -> x0, local copies, waits for them, and re-layouts: 19 us -> none  [the longest x1 4.72 us: per_device(): lax.all_gather(audio_self_value[0], 'seq', axis=0, tiled=True)]
  transfers between devices with their start and end apart: 8 -> 0, of which waited for: 2 -> 0; matrix products, arithmetic and copies ran while one was open for 9% -> 0% of each run, Pallas kernels for 0% -> 0%
where the time goes in v2:
time: 47 us; the launch traced here: 46.9 us
  Pallas kernels  46.3 us (99%)
  between operations  0.65 us (1%)
    pallas_call x1, Pallas kernels, per_device(): pl.pallas_call(kernel, out_shape=(jax.ShapeDtypeStruct((4, 64, GW), bf16)...  44.7 us
    pallas_call x1, Pallas kernels, per_device(): pl.pallas_call(guide_kernel, out_shape=(jax.ShapeDtypeStruct((64, 2 * GW)...  1.61 us

profile of v2, /device:TPU:1, one launch (start us, length us, event | category | flops | bytes accessed | tf_op | source)
XLA Modules:
  0.0 46.9 jit_solution(18364042906492254792)
XLA Ops:
  0.6 44.7 %shard_map.203 = (bf16[4,64,384]{2,1,0:T(8,128)(2,1)}, f32[4,8,384]{2,1,0:T(8,128)}) custom-call(bf16[1,64,3072]{2,1,0:T(8,128)(2,1)} %hidden_hbm.1, bf16[3072,1536]{1,0:T(8,128)(2,1)} %weight.1, bf16[1,64,1536]{2,1,0:T(8,128)(2,1)} %video_key_hbm.1, bf16[1,64,1536]{2,1,0:T(8,128)(2,1)} %video_value.1, bf16[1,8,1536]{2,1,0:T(8,128)(2,1)} %cross_key_hbm.1, ...), custom_call_target="tpu_custom_call" | custom-call | flops 1811939328 | bytes 12000000 | tf_op jit(solution)/shard_map/pallas_call | solution.py:687
  45.3 1.6 %shard_map.204 = (bf16[64,768]{1,0:T(8,128)(2,1)}, bf16[8,768]{1,0:T(8,128)(2,1)}) custom-call(bf16[4,64,384]{2,1,0:T(8,128)(2,1)} %get-tuple-element.4.video, f32[4,8,384]{2,1,0:T(8,128)} %get-tuple-element.5.audio), custom_call_target="tpu_custom_call" | custom-call | tf_op jit(solution)/shard_map/pallas_call | solution.py:757

commit v3 on v0

v3 whole, which is shorter than its diff:
```python
import math

import jax
import jax.numpy as jnp
import numpy as np
from jax import lax
from jax.experimental import pallas as pl
from jax.experimental.pallas import tpu as pltpu
from jax.sharding import PartitionSpec as P

HEADS = 12
HEAD_DIM = 128
MESH = pl.DeviceIdType.MESH

epsilon = 1e-06
rope_base = 10000.0
guide_scale = 3.0

GROUP = 3
GW = GROUP * HEAD_DIM
CK, CV, KEEP, KV_LANES = 0, 384, 768, 896
SCORE_SCALE = math.log2(math.e) / math.sqrt(HEAD_DIM)
NT = (((1,), (1,)), ((), ()))


def rope_heads(items):
    means = [jnp.mean(rows * rows, axis=1, keepdims=True) for rows, _, _, _ in items]
    scaled = [
        rows * lax.rsqrt(mean + epsilon) * gain
        for mean, (rows, gain, _, _) in zip(means, items)
    ]
    turned = [pltpu.roll(one, 64, 1) for one in scaled]
    return [
        one * cos + other * sin
        for one, other, (_, _, cos, sin) in zip(scaled, turned, items)
    ]


def weigh(queries, keys, values):
    scores = lax.dot_general(queries, keys, NT, preferred_element_type=jnp.float32)
    weights = jnp.exp2(scores * SCORE_SCALE).astype(jnp.bfloat16)
    return jnp.dot(weights, values, preferred_element_type=jnp.float32)


def head(index, base=0):
    return slice(base + index * HEAD_DIM, base + (index + 1) * HEAD_DIM)


TRANSFERS = (
    "z1",
    "z2",
    "zk",
    "zv",
    "zq",
    "g0ax",
    "g0by",
    "g0ay",
    "g0bx",
    "g1ax",
    "g1by",
    "g1ay",
    "g1bx",
    "sqx",
    "sky",
    "sib_k",
    "sib_v",
    "sib_s",
    "sib_g",
    "rs",
    "ss",
    "vf",
    "af",
    "vf_near",
    "af_near",
)
SEM = {name: n for n, name in enumerate(TRANSFERS)}


def kernel(
    hidden_hbm,
    weight,
    video_key_hbm,
    video_value,
    cross_key_hbm,
    cross_value_hbm,
    audio_query_hbm,
    self_query_hbm,
    self_key_hbm,
    self_value_hbm,
    v2a_qgain_hbm,
    v2a_kgain_hbm,
    self_qgain_hbm,
    self_kgain_hbm,
    a2v_qgain_hbm,
    a2v_kgain_hbm,
    video_time,
    audio_time,
    branch_keep,
    frequency,
    vfin,
    afin,
    hidden_in,
    key_in,
    audio_in,
    gain_in,
    frequency_in,
    video_clock,
    audio_clock,
    keep_in,
    in_sem,
    wbuf,
    stage1,
    stage2,
    recv1,
    recv2,
    g0,
    g1,
    squery,
    sblock,
    spartial,
    spartials,
    vq_send,
    vk_send,
    vq,
    vk,
    vv,
    partial,
    partials,
    vpart,
    apart,
    send_sem,
    recv_sem,
):
    cfg = lax.axis_index("cfg")
    seq = lax.axis_index("seq")
    core = lax.rem(seq, 2)
    y = lax.rem(seq // 2, 4)
    zh = lax.rem(seq // 8, 4)
    x = seq // 32

    def plus(value, d):
        return lax.rem(value + 4 + d, 4)

    def device(cfg_, x_, zh_, y_, core_):
        return (cfg_, ((x_ * 4 + zh_) * 4 + y_) * 2 + core_)

    def group_of(z):
        return lax.rem(z, 2) * 2 + z // 2

    def at(dx=0, dy=0, dz=0):
        return device(cfg, plus(x, dx), plus(zh, dz), plus(y, dy), core)

    sibling = device(cfg, x, zh, y, 1 - core)

    def remote(src, dst, name, target):
        return pltpu.make_async_remote_copy(
            src_ref=src,
            dst_ref=dst,
            send_sem=send_sem.at[SEM[name]],
            recv_sem=recv_sem.at[SEM[name]],
            device_id=target,
            device_id_type=MESH,
        )

    def start(src, dst, name, target):
        remote(src, dst, name, target).start()

    def arrived(ref, name):
        remote(ref, ref, name, sibling).wait_recv()

    def sent(ref, name):
        remote(ref, ref, name, sibling).wait_send()

    def rows(first, count):
        return pl.ds(first, count)

    barrier = pltpu.get_barrier_semaphore()
    peers = [sibling]
    for dx in range(4):
        for dy in range(4):
            if dx or dy:
                peers.append(at(dx=dx, dy=dy))
    for d in range(4):
        if d:
            peers.append(at(dz=d))
        peers.append(device(1 - cfg, x, plus(zh, d), y, core))
    for peer in peers:
        pl.semaphore_signal(barrier, inc=1, device_id=peer, device_id_type=MESH)

    first_inputs = [
        (audio_time, audio_clock, 0),
        (branch_keep.at[0], keep_in, 1),
        (frequency, frequency_in, 2),
        (a2v_qgain_hbm, gain_in.at[0], 3),
        (v2a_kgain_hbm, gain_in.at[1], 4),
    ]
    second_inputs = [(self_qgain_hbm, gain_in.at[2], 5), (self_kgain_hbm, gain_in.at[3], 6)]
    video_inputs = [
        (video_time, video_clock, 7),
        (video_key_hbm.at[0], key_in, 8),
        (a2v_kgain_hbm, gain_in.at[4], 9),
    ]
    query_inputs = [(v2a_qgain_hbm, gain_in.at[5], 10), (hidden_hbm.at[0], hidden_in, 11)]
    audio_inputs = [
        (audio_query_hbm.at[0], audio_in.at[0], 12),
        (cross_key_hbm.at[0], audio_in.at[1], 12),
        (cross_value_hbm.at[0], audio_in.at[2], 12),
        (self_query_hbm.at[0], audio_in.at[3], 13),
        (self_key_hbm.at[0], audio_in.at[4], 13),
        (self_value_hbm.at[0], audio_in.at[5], 13),
    ]

    def local(entry):
        src, dst, n = entry
        return pltpu.make_async_copy(src, dst, in_sem.at[n])

    for entry in first_inputs + audio_inputs + second_inputs + video_inputs + query_inputs:
        local(entry).start()

    for n in range(6):
        local((weight.at[:, pl.ds(n * 256, 256)], wbuf.at[n], 14)).start()

    def spread(scalars, count):
        row = lax.broadcasted_iota(jnp.int32, (8, HEAD_DIM), 0)
        tiles = []
        for first in range(0, count, 8):
            tile = jnp.zeros((8, HEAD_DIM), jnp.int32)
            for r in range(8):
                tile = jnp.where(row == r, scalars[first + r], tile)
            tiles.append(tile)
        return jnp.concatenate(tiles, axis=0).astype(jnp.float32)

    def tables(scalars, count):
        angles = spread(scalars, count) * frequency_in[...]
        lanes = lax.broadcasted_iota(jnp.int32, (count, HEAD_DIM), 1)
        sin = jnp.sin(angles)
        return jnp.cos(angles), jnp.where(lanes < HEAD_DIM // 2, -sin, sin)

    def gain(which, h):
        return gain_in[which, head(h)].reshape(1, HEAD_DIM)

    def audio_rows(which, h):
        return audio_in[which, :, head(h)].astype(jnp.float32)

    def wait_audio(group):
        three = audio_in.at[pl.ds(3 * group, 3)]
        local((three, three, 12 + group)).wait()

    for entry in first_inputs:
        local(entry).wait()
    wait_audio(0)
    acos, asin = tables(audio_clock, 8)
    mask = spread(keep_in, 8)
    nothing = jnp.zeros((8, HEAD_DIM), jnp.float32)

    def stage(ref, base, last):
        ropes = rope_heads(
            [
                (audio_rows(base + n, h), gain(base // 3 * 2 + n, h), acos, asin)
                for n in range(2)
                for h in range(HEADS)
            ]
        )
        values = [audio_rows(base + 2, h) * mask for h in range(HEADS)]
        for group in range(4):
            of = slice(group * GROUP, (group + 1) * GROUP)
            pieces = ropes[:HEADS][of] + ropes[HEADS:][of] + values[of] + [last]
            halves = [jnp.concatenate(pieces[n : n + 5], axis=1) for n in (0, 5)]
            ref[group] = jnp.concatenate(halves, axis=0).astype(jnp.bfloat16)

    stage(stage1, 0, mask)
    pl.semaphore_wait(barrier, len(peers))
    for d in (2, 1, 3):
        start(stage1.at[group_of(plus(zh, d))], recv1.at[d], "z1", at(dz=d))
    recv1[0] = stage1[group_of(zh)]

    for entry in second_inputs:
        local(entry).wait()
    wait_audio(1)
    stage(stage2, 3, nothing)
    for d in (2, 1, 3):
        start(stage2.at[group_of(plus(zh, d))], recv2.at[d], "z2", at(dz=d))
    recv2[0] = stage2[group_of(zh)]

    for entry in video_inputs:
        local(entry).wait()
    vcos, vsin = tables(video_clock, 64)
    for first in range(0, HEADS, 4):
        ropes = rope_heads(
            [
                (key_in[:, head(h)].astype(jnp.float32), gain(4, h), vcos, vsin)
                for h in range(first, first + 4)
            ]
        )
        vk_send[:, first * HEAD_DIM : (first + 4) * HEAD_DIM] = jnp.concatenate(
            ropes, axis=1
        ).astype(jnp.bfloat16)

    def lanes_of(z):
        return pl.ds(pl.multiple_of(group_of(z) * GW, 128), GW)

    for d in (2, 1, 3):
        start(vk_send.at[:, lanes_of(plus(zh, d))], vk.at[rows(64 * d, 64)], "zk", at(dz=d))
        start(
            video_value.at[0, :, lanes_of(plus(zh, d))], vv.at[rows(64 * d, 64)], "zv", at(dz=d)
        )
    own_value = local((video_value.at[0, :, lanes_of(zh)], vv.at[rows(0, 64)], 15))
    own_value.start()
    vk[0:64] = vk_send[:, lanes_of(zh)]

    for entry in query_inputs:
        local(entry).wait()
    local((wbuf, wbuf, 14)).wait()

    def project(chunks):
        products = [
            jnp.dot(hidden_in[...], wbuf[n], preferred_element_type=jnp.float32)
            for n in chunks
        ]
        ropes = rope_heads(
            [
                (products[i][:, head(part)], gain(5, 2 * n + part), vcos, vsin)
                for i, n in enumerate(chunks)
                for part in range(2)
            ]
        )
        for i, n in enumerate(chunks):
            vq_send[:, 256 * n : 256 * n + 256] = jnp.concatenate(
                ropes[2 * i : 2 * i + 2], axis=1
            ).astype(jnp.bfloat16)

    for chunks in ((0, 1), (2, 3), (4, 5)):
        project(chunks)
    vq[0:64] = vq_send[:, lanes_of(zh)]

    def rows_of(recv):
        received = [recv[d].astype(jnp.float32) for d in range(4)]

        def piece(n):
            row, lane = 8 * (n // 5), n % 5 * HEAD_DIM
            return jnp.concatenate(
                [one[row : row + 8, lane : lane + HEAD_DIM] for one in received], axis=0
            )

        pieces = [piece(n).astype(jnp.bfloat16) for n in range(10)]
        return [
            jnp.concatenate(pieces[n : n + GROUP], axis=1) for n in range(0, 9, GROUP)
        ] + pieces[9:]

    def place(ref, lane, block):
        lanes = slice(lane, lane + block.shape[1])
        ref[0:16, lanes] = block[:16]
        ref[256:272, lanes] = block[16:]

    def first_phase(ref, name):
        for d in (2, 1, 3):
            start(ref.at[rows(0, 16)], ref.at[rows(16 * d, 16)], name + "ax", at(dx=d))
            start(ref.at[rows(256, 16)], ref.at[rows(256 + 16 * d, 16)], name + "by", at(dy=d))

    def second_phase(ref, name):
        arrived(ref.at[rows(16, 48)], name + "ax")
        arrived(ref.at[rows(272, 48)], name + "by")
        for d in (2, 1, 3):
            start(ref.at[rows(0, 64)], ref.at[rows(64 * d, 64)], name + "ay", at(dy=d))
            start(ref.at[rows(256, 64)], ref.at[rows(256 + 64 * d, 64)], name + "bx", at(dx=d))

    def gathered(ref, name):
        arrived(ref.at[rows(64, 192)], name + "ay")
        arrived(ref.at[rows(320, 192)], name + "bx")

    arrived(recv1.at[rows(1, 3)], "z1")
    queries, keys, values, kept = rows_of(recv1)
    place(g0, 0, queries)
    first_phase(g0, "g0")
    place(g1, CK, keys)
    place(g1, CV, values)
    place(g1, KEEP, kept)
    first_phase(g1, "g1")

    arrived(recv2.at[rows(1, 3)], "z2")
    queries, keys, values, _ = rows_of(recv2)
    squery[0:32] = queries
    sblock[0:32, CK : CK + GW] = keys
    sblock[0:32, CV : CV + GW] = values
    sblock[0:32, KEEP : KEEP + HEAD_DIM] = kept
    for d in (2, 1, 3):
        start(squery.at[rows(0, 32)], squery.at[rows(32 * d, 32)], "sqx", at(dx=d))
        start(sblock.at[rows(0, 32)], sblock.at[rows(32 * d, 32)], "sky", at(dy=d))

    for d in (2, 1, 3):
        start(vq_send.at[:, lanes_of(plus(zh, d))], vq.at[rows(64 * d, 64)], "zq", at(dz=d))

    second_phase(g0, "g0")
    second_phase(g1, "g1")

    arrived(sblock.at[rows(32, 96)], "sky")
    start(sblock.at[rows(0, 128)], sblock.at[rows(128, 128)], "sib_s", sibling)

    lane = lax.broadcasted_iota(jnp.int32, (16, HEAD_DIM), 1)
    lane_group = lax.rem(lane, 64) // 8

    def pack(ref, slot, results, first, second):
        halves = []
        for start_row in (first, second):
            totals = jnp.zeros((16, HEAD_DIM), jnp.float32)
            for h, both in enumerate(results):
                total = both[start_row : start_row + 16, HEAD_DIM:]
                high = total.astype(jnp.bfloat16).astype(jnp.float32)
                totals = jnp.where(lane_group == 2 * h, high, totals)
                totals = jnp.where(lane_group == 2 * h + 1, total - high, totals)
            halves.append(totals)
        for h, both in enumerate(results):
            for n, start_row in enumerate((first, second)):
                ref[slot, 32 * h + 16 * n : 32 * h + 16 * n + 16] = both[
                    start_row : start_row + 16, :HEAD_DIM
                ].astype(jnp.bfloat16)
        ref[slot, 96:112] = jnp.where(lane < 64, halves[0], halves[1]).astype(jnp.bfloat16)

    own_value.wait()
    arrived(vk.at[rows(64, 192)], "zk")
    arrived(vv.at[rows(64, 192)], "zv")
    start(vk.at[rows(0, 256)], vk.at[rows(256, 256)], "sib_k", sibling)
    start(vv.at[rows(0, 256)], vv.at[rows(256, 256)], "sib_v", sibling)
    gathered(g0, "g0")
    ones = jnp.ones((256, HEAD_DIM), jnp.bfloat16)

    def audio_over_video(pair, h, first):
        queries = []
        for dx in pair:
            for dy in range(4):
                row = (4 * dy + dx) * 16
                queries.append(g0[row : row + 16, head(h)])
            row = 256 + 64 * dx
            queries.append(g0[row : row + 64, head(h)])
        return weigh(
            jnp.concatenate(queries, axis=0),
            vk[first : first + 256, head(h)],
            jnp.concatenate([vv[first : first + 256, head(h)], ones], axis=1),
        )

    pairs = ((2, 1), (3, 0))
    near = [[audio_over_video(pair, h, 0) for h in range(GROUP)] for pair in pairs]

    arrived(squery.at[rows(32, 96)], "sqx")
    arrived(sblock.at[rows(128, 128)], "sib_s")
    results = [
        weigh(
            squery[:, head(h)],
            sblock[:, head(h, CK)],
            jnp.concatenate([sblock[:, head(h, CV)], sblock[:, KEEP:KV_LANES]], axis=1),
        )
        for h in range(GROUP)
    ]
    for dx in (2, 1, 3, 0):
        if dx:
            pack(spartial, dx, results, 32 * dx, 32 * dx + 16)
            start(spartial.at[dx], spartials.at[dx], "ss", at(dx=-dx))
        else:
            pack(spartials, dx, results, 32 * dx, 32 * dx + 16)

    arrived(vk.at[rows(256, 256)], "sib_k")
    arrived(vv.at[rows(256, 256)], "sib_v")
    summed = [
        [near_results[h] + audio_over_video(pair, h, 256) for h in range(GROUP)]
        for pair, near_results in zip(pairs, near)
    ]
    for pair, results in zip(pairs, summed):
        for n, dx in enumerate(pair):
            for dy in (2, 1, 3, 0):
                slot = 4 * dx + dy
                row = 128 * n + 16 * dy
                if slot:
                    pack(partial, slot, results, row, row + 64)
                    start(partial.at[slot], partials.at[slot], "rs", at(dx=-dx, dy=-dy))
                else:
                    pack(partials, slot, results, row, row + 64)

    gathered(g1, "g1")
    start(g1.at[rows(0, 512)], g1.at[rows(512, 512)], "sib_g", sibling)
    arrived(vq.at[rows(64, 192)], "zq")

    def video_over_audio(pair, h, first):
        return weigh(
            jnp.concatenate([vq[64 * d : 64 * d + 64, head(h)] for d in pair], axis=0),
            g1[first : first + 512, head(h, CK)],
            jnp.concatenate(
                [g1[first : first + 512, head(h, CV)], g1[first : first + 512, KEEP:KV_LANES]],
                axis=1,
            ),
        )

    final_cfg = lax.rem(zh, 2)
    is_final = cfg == final_cfg
    slot_out = cfg * 2 + zh // 2

    def final(src, dst, name, d):
        target = device(final_cfg, x, plus(zh, -d), y, core)
        if d:
            start(src, dst, name, target)
        else:
            near_copy = pltpu.make_async_remote_copy(
                src_ref=src,
                dst_ref=dst,
                send_sem=send_sem.at[SEM[name + "_near"]],
                recv_sem=recv_sem.at[SEM[name]],
                device_id=target,
                device_id_type=MESH,
            )
            here_copy = pltpu.make_async_copy(src, dst, recv_sem.at[SEM[name]])
            pl.when(jnp.logical_not(is_final))(near_copy.start)
            pl.when(is_final)(here_copy.start)

    near = [[video_over_audio(pair, h, 0) for h in range(GROUP)] for pair in pairs]
    arrived(g1.at[rows(512, 512)], "sib_g")
    summed = [
        [near_results[h] + video_over_audio(pair, h, 512) for h in range(GROUP)]
        for pair, near_results in zip(pairs, near)
    ]
    for pair, results in zip(pairs, summed):
        for h, both in enumerate(results):
            done = (both[:, :HEAD_DIM] / both[:, HEAD_DIM:]).astype(jnp.bfloat16)
            for n, d in enumerate(pair):
                vpart[64 * d : 64 * d + 64, head(h)] = done[64 * n : 64 * n + 64]
        for d in pair:
            final(vpart.at[rows(64 * d, 64)], vfin.at[slot_out], "vf", d)

    def quotients(ref, count):
        summed = ref[0].astype(jnp.float32)
        for n in range(1, count):
            summed = summed + ref[n].astype(jnp.float32)
        tile = summed[96:112]
        result = []
        for h in range(GROUP):
            totals = [
                tile[:, first : first + 1] + tile[:, first + 8 : first + 9]
                for first in (16 * h, 64 + 16 * h)
            ]
            result.append(summed[32 * h : 32 * h + 32] / jnp.concatenate(totals, axis=0))
        return jnp.concatenate(result, axis=1)

    arrived(spartials.at[rows(1, 3)], "ss")
    self_part = quotients(spartials, 4)
    arrived(partials.at[rows(1, 15)], "rs")
    part = self_part + quotients(partials, 16)
    apart[...] = part.astype(jnp.bfloat16).astype(jnp.float32)
    for d in (2, 1, 3, 0):
        final(apart.at[rows(8 * d, 8)], afin.at[slot_out], "af", d)

    for name in ("z1", "z2"):
        sent(stage1.at[rows(0, 3)], name)
    for name in ("zk", "zv", "zq"):
        sent(vk.at[rows(0, 192)], name)
    for name, ref in (("g0", g0), ("g1", g1)):
        for kind, count in (("ax", 48), ("by", 48), ("ay", 192), ("bx", 192)):
            sent(ref.at[rows(0, count)], name + kind)
    sent(squery.at[rows(0, 96)], "sqx")
    sent(sblock.at[rows(0, 96)], "sky")
    sent(vk.at[rows(0, 256)], "sib_k")
    sent(vv.at[rows(0, 256)], "sib_v")
    sent(sblock.at[rows(0, 128)], "sib_s")
    sent(g1.at[rows(0, 512)], "sib_g")
    sent(partial.at[rows(1, 15)], "rs")
    sent(spartial.at[rows(1, 3)], "ss")
    sent(vpart.at[rows(64, 192)], "vf")
    sent(apart.at[rows(8, 24)], "af")

    @pl.when(jnp.logical_not(is_final))
    def _():
        sent(vpart.at[rows(0, 64)], "vf_near")
        sent(apart.at[rows(0, 8)], "af_near")

    arrived(vfin, "vf")
    arrived(afin, "af")


def guide_kernel(video, audio, video_out, audio_out):
    def guide(cond, uncond):
        uncond = uncond.astype(jnp.float32)
        return (uncond + guide_scale * (cond.astype(jnp.float32) - uncond)).astype(
            jnp.bfloat16
        )

    for j in range(2):
        video_out[:, j * GW : (j + 1) * GW] = guide(video[j], video[2 + j])
    audio_out[...] = jnp.concatenate(
        [guide(audio[j], audio[2 + j]) for j in range(2)], axis=1
    )


def per_device(
    video_hidden,
    video_weight,
    video_key,
    video_value,
    audio_cross_key,
    audio_cross_value,
    audio_query,
    audio_self_query,
    audio_self_key,
    audio_self_value,
    v2a_qgain,
    v2a_kgain,
    self_qgain,
    self_kgain,
    a2v_qgain,
    a2v_kgain,
    video_time,
    audio_time,
    branch_keep,
):
    half_dim = HEAD_DIM // 2
    steps = np.arange(half_dim, dtype=np.float32) / np.float32(half_dim)
    frequencies = np.float32(rope_base) ** -steps
    frequencies = np.concatenate([frequencies, frequencies]).reshape(1, HEAD_DIM)

    vmem = pl.BlockSpec(memory_space=pltpu.VMEM)
    bf16, f32 = jnp.bfloat16, jnp.float32
    dma = pltpu.SemaphoreType.DMA
    hbm = pl.BlockSpec(memory_space=pltpu.HBM)
    parts = pl.pallas_call(
        kernel,
        out_shape=(
            jax.ShapeDtypeStruct((4, 64, GW), bf16),
            jax.ShapeDtypeStruct((4, 8, GW), f32),
        ),
        in_specs=[hbm] * 20,
        out_specs=(hbm, hbm),
        scratch_shapes=[
            pltpu.VMEM((64, 3072), bf16),
            pltpu.VMEM((64, 4 * GW), bf16),
            pltpu.VMEM((6, 8, 4 * GW), bf16),
            pltpu.VMEM((6, 4 * GW), f32),
            pltpu.VMEM((1, HEAD_DIM), f32),
            pltpu.SMEM((64,), jnp.int32),
            pltpu.SMEM((8,), jnp.int32),
            pltpu.SMEM((8,), jnp.int32),
            dma((16,)),
            pltpu.VMEM((6, 3072, 256), bf16),
            pltpu.VMEM((4, 16, 5 * HEAD_DIM), bf16),
            pltpu.VMEM((4, 16, 5 * HEAD_DIM), bf16),
            pltpu.VMEM((4, 16, 5 * HEAD_DIM), bf16),
            pltpu.VMEM((4, 16, 5 * HEAD_DIM), bf16),
            pltpu.VMEM((512, GW), bf16),
            pltpu.VMEM((1024, KV_LANES), bf16),
            pltpu.VMEM((128, GW), bf16),
            pltpu.VMEM((256, KV_LANES), bf16),
            pltpu.VMEM((4, 112, HEAD_DIM), bf16),
            pltpu.VMEM((4, 112, HEAD_DIM), bf16),
            pltpu.VMEM((64, 4 * GW), bf16),
            pltpu.VMEM((64, 4 * GW), bf16),
            pltpu.VMEM((256, GW), bf16),
            pltpu.VMEM((512, GW), bf16),
            pltpu.VMEM((512, GW), bf16),
            pltpu.VMEM((16, 112, HEAD_DIM), bf16),
            pltpu.VMEM((16, 112, HEAD_DIM), bf16),
            pltpu.VMEM((256, GW), bf16),
            pltpu.VMEM((32, GW), f32),
            dma((len(TRANSFERS),)),
            dma((len(TRANSFERS),)),
        ],
        compiler_params=pltpu.CompilerParams(
            collective_id=0, has_side_effects=True, vmem_limit_bytes=64 * 1024 * 1024
        ),
        cost_estimate=pl.CostEstimate(
            flops=2 * 64 * 3072 * 1536 * 3, bytes_accessed=12_000_000, transcendentals=1_700_000
        ),
    )(
        video_hidden,
        video_weight,
        video_key,
        video_value,
        audio_cross_key,
        audio_cross_value,
        audio_query,
        audio_self_query,
        audio_self_key,
        audio_self_value,
        v2a_qgain,
        v2a_kgain,
        self_qgain,
        self_kgain,
        a2v_qgain,
        a2v_kgain,
        video_time,
        audio_time,
        branch_keep,
        frequencies,
    )
    return pl.pallas_call(
        guide_kernel,
        out_shape=(
            jax.ShapeDtypeStruct((64, 2 * GW), bf16),
            jax.ShapeDtypeStruct((8, 2 * GW), bf16),
        ),
        in_specs=[vmem, vmem],
        out_specs=(vmem, vmem),
    )(*parts)


def solution(mesh):
    in_specs = (
        P("cfg", "seq", None),
        P(),
        P("cfg", "seq", None),
        P("cfg", "seq", None),
        P("cfg", "seq", None),
        P("cfg", "seq", None),
        P("cfg", "seq", None),
        P("cfg", "seq", None),
        P("cfg", "seq", None),
        P("cfg", "seq", None),
        P(),
        P(),
        P(),
        P(),
        P(),
        P(),
        P("seq"),
        P("seq"),
        P("cfg", "seq"),
    )
    out_specs = (P("seq", "cfg"), P("seq", "cfg"))
    return jax.shard_map(
        per_device, mesh=mesh, in_specs=in_specs, out_specs=out_specs, check_vma=False
    )
```

time: 1840 us -> 44.6 us (0.02)
  blocking collectives: 1030 us -> 0 us
  waiting for transfers between devices: 590 us -> 0 us
  matrix products: 87.6 us -> 0 us
  local copies, waits for them, and re-layouts: 63.1 us -> 0 us
  Pallas kernels: 0 us -> 43.9 us
  other arithmetic: 31.5 us -> 0 us
    psum x1 -> x0, blocking collectives: 685 us -> none  [per_device(): summed_num, summed_tot = lax.psum((numerator, totals), 'seq')]
    psum x1 -> x0, waiting for transfers between devices: 586 us -> none  [per_device(): summed_num, summed_tot = lax.psum((numerator, totals), 'seq')]
    unnamed x1 -> x0, blocking collectives: 349 us -> none
    dot_general x73 -> x0, matrix products: 87.6 us -> none  [the longest x24 34.6 us: attend_one_head(): jnp.dot(weights.astype(jnp.bfloat16), head_value, preferred_element_type=...]
    pallas_call x0 -> x2, Pallas kernels: none -> 43.9 us  [the longest x1 42.3 us: per_device(): pl.pallas_call(kernel, out_shape=(jax.ShapeDtypeStruct((4, 64, GW), bf16)...]
    all_gather x5 -> x0, local copies, waits for them, and re-layouts: 19 us -> none  [the longest x1 4.72 us: per_device(): lax.all_gather(audio_self_value[0], 'seq', axis=0, tiled=True)]
  transfers between devices with their start and end apart: 8 -> 0, of which waited for: 2 -> 0; matrix products, arithmetic and copies ran while one was open for 9% -> 0% of each run, Pallas kernels for 0% -> 0%
where the time goes in v3:
time: 44.6 us; the launch traced here: 44.5 us
  Pallas kernels  43.9 us (98%)
  between operations  0.65 us (1%)
    pallas_call x1, Pallas kernels, per_device(): pl.pallas_call(kernel, out_shape=(jax.ShapeDtypeStruct((4, 64, GW), bf16)...  42.3 us
    pallas_call x1, Pallas kernels, per_device(): pl.pallas_call(guide_kernel, out_shape=(jax.ShapeDtypeStruct((64, 2 * GW)...  1.61 us

profile of v3, /device:TPU:1, one launch (start us, length us, event | category | flops | bytes accessed | tf_op | source)
XLA Modules:
  0.0 44.5 jit_solution(15103837749236047961)
XLA Ops:
  0.6 42.3 %shard_map.203 = (bf16[4,64,384]{2,1,0:T(8,128)(2,1)}, f32[4,8,384]{2,1,0:T(8,128)}) custom-call(bf16[1,64,3072]{2,1,0:T(8,128)(2,1)} %hidden_hbm.1, bf16[3072,1536]{1,0:T(8,128)(2,1)} %weight.1, bf16[1,64,1536]{2,1,0:T(8,128)(2,1)} %video_key_hbm.1, bf16[1,64,1536]{2,1,0:T(8,128)(2,1)} %video_value.1, bf16[1,8,1536]{2,1,0:T(8,128)(2,1)} %cross_key_hbm.1, ...), custom_call_target="tpu_custom_call" | custom-call | flops 1811939328 | bytes 12000000 | tf_op jit(solution)/shard_map/pallas_call | solution.py:620
  42.9 1.6 %shard_map.204 = (bf16[64,768]{1,0:T(8,128)(2,1)}, bf16[8,768]{1,0:T(8,128)(2,1)}) custom-call(bf16[4,64,384]{2,1,0:T(8,128)(2,1)} %get-tuple-element.4.video, f32[4,8,384]{2,1,0:T(8,128)} %get-tuple-element.5.audio), custom_call_target="tpu_custom_call" | custom-call | tf_op jit(solution)/shard_map/pallas_call | solution.py:689

commit v4 on v3

--- a/solution.py
+++ b/solution.py
@@ -52,10 +52,7 @@
     "zk",
     "zv",
     "zq",
-    "g0ax",
-    "g0by",
-    "g0ay",
-    "g0bx",
+    "g0",
     "g1ax",
     "g1by",
     "g1ay",
@@ -299,11 +296,14 @@
     def lanes_of(z):
         return pl.ds(pl.multiple_of(group_of(z) * GW, 128), GW)
 
-    for d in (2, 1, 3):
-        start(vk_send.at[:, lanes_of(plus(zh, d))], vk.at[rows(64 * d, 64)], "zk", at(dz=d))
-        start(
-            video_value.at[0, :, lanes_of(plus(zh, d))], vv.at[rows(64 * d, 64)], "zv", at(dz=d)
-        )
+    def send_keys_values():
+        for d in (2, 1, 3):
+            start(vk_send.at[:, lanes_of(plus(zh, d))], vk.at[rows(64 * d, 64)], "zk", at(dz=d))
+            start(
+                video_value.at[0, :, lanes_of(plus(zh, d))], vv.at[rows(64 * d, 64)], "zv", at(dz=d)
+            )
+
+    pl.when(core == 0)(send_keys_values)
     own_value = local((video_value.at[0, :, lanes_of(zh)], vv.at[rows(0, 64)], 15))
     own_value.start()
     vk[0:64] = vk_send[:, lanes_of(zh)]
@@ -331,6 +331,7 @@
 
     for chunks in ((0, 1), (2, 3), (4, 5)):
         project(chunks)
+    pl.when(core == 1)(send_keys_values)
     vq[0:64] = vq_send[:, lanes_of(zh)]
 
     def rows_of(recv):
@@ -370,12 +371,20 @@
 
     arrived(recv1.at[rows(1, 3)], "z1")
     queries, keys, values, kept = rows_of(recv1)
-    place(g0, 0, queries)
-    first_phase(g0, "g0")
     place(g1, CK, keys)
     place(g1, CV, values)
     place(g1, KEEP, kept)
     first_phase(g1, "g1")
+    g0[0:32] = queries
+    for dx in (2, 1, 3, 0):
+        for dy in (2, 1, 3, 0):
+            if dx or dy:
+                start(
+                    g0.at[rows(0, 32)],
+                    g0.at[rows(32 * (4 * dx + dy), 32)],
+                    "g0",
+                    at(dx=dx, dy=dy),
+                )
 
     arrived(recv2.at[rows(1, 3)], "z2")
     queries, keys, values, _ = rows_of(recv2)
@@ -387,14 +396,10 @@
         start(squery.at[rows(0, 32)], squery.at[rows(32 * d, 32)], "sqx", at(dx=d))
         start(sblock.at[rows(0, 32)], sblock.at[rows(32 * d, 32)], "sky", at(dy=d))
 
+    second_phase(g1, "g1")
+
     for d in (2, 1, 3):
         start(vq_send.at[:, lanes_of(plus(zh, d))], vq.at[rows(64 * d, 64)], "zq", at(dz=d))
-
-    second_phase(g0, "g0")
-    second_phase(g1, "g1")
-
-    arrived(sblock.at[rows(32, 96)], "sky")
-    start(sblock.at[rows(0, 128)], sblock.at[rows(128, 128)], "sib_s", sibling)
 
     lane = lax.broadcasted_iota(jnp.int32, (16, HEAD_DIM), 1)
     lane_group = lax.rem(lane, 64) // 8
@@ -421,17 +426,11 @@
     arrived(vv.at[rows(64, 192)], "zv")
     start(vk.at[rows(0, 256)], vk.at[rows(256, 256)], "sib_k", sibling)
     start(vv.at[rows(0, 256)], vv.at[rows(256, 256)], "sib_v", sibling)
-    gathered(g0, "g0")
+    arrived(g0.at[rows(32, 480)], "g0")
     ones = jnp.ones((256, HEAD_DIM), jnp.bfloat16)
 
     def audio_over_video(pair, h, first):
-        queries = []
-        for dx in pair:
-            for dy in range(4):
-                row = (4 * dy + dx) * 16
-                queries.append(g0[row : row + 16, head(h)])
-            row = 256 + 64 * dx
-            queries.append(g0[row : row + 64, head(h)])
+        queries = [g0[128 * dx : 128 * dx + 128, head(h)] for dx in pair]
         return weigh(
             jnp.concatenate(queries, axis=0),
             vk[first : first + 256, head(h)],
@@ -441,6 +440,62 @@
     pairs = ((2, 1), (3, 0))
     near = [[audio_over_video(pair, h, 0) for h in range(GROUP)] for pair in pairs]
 
+    arrived(vk.at[rows(256, 256)], "sib_k")
+    arrived(vv.at[rows(256, 256)], "sib_v")
+    summed = [
+        [near_results[h] + audio_over_video(pair, h, 256) for h in range(GROUP)]
+        for pair, near_results in zip(pairs, near)
+    ]
+    for pair, results in zip(pairs, summed):
+        for n, dx in enumerate(pair):
+            for dy in (2, 1, 3, 0):
+                slot = 4 * dx + dy
+                row = 128 * n + 32 * dy
+                if slot:
+                    pack(partial, slot, results, row, row + 16)
+                    start(partial.at[slot], partials.at[slot], "rs", at(dx=-dx, dy=-dy))
+                else:
+                    pack(partials, slot, results, row, row + 16)
+
+    arrived(sblock.at[rows(32, 96)], "sky")
+    start(sblock.at[rows(0, 128)], sblock.at[rows(128, 128)], "sib_s", sibling)
+
+    gathered(g1, "g1")
+    start(g1.at[rows(0, 512)], g1.at[rows(512, 512)], "sib_g", sibling)
+    arrived(vq.at[rows(64, 192)], "zq")
+
+    def video_over_audio(pair, h, first):
+        return weigh(
+            jnp.concatenate([vq[64 * d : 64 * d + 64, head(h)] for d in pair], axis=0),
+            g1[first : first + 512, head(h, CK)],
+            jnp.concatenate(
+                [g1[first : first + 512, head(h, CV)], g1[first : first + 512, KEEP:KV_LANES]],
+                axis=1,
+            ),
+        )
+
+    final_cfg = lax.rem(zh, 2)
+    is_final = cfg == final_cfg
+    slot_out = cfg * 2 + zh // 2
+
+    def final(src, dst, name, d):
+        target = device(final_cfg, x, plus(zh, -d), y, core)
+        if d:
+            start(src, dst, name, target)
+        else:
+            near_copy = pltpu.make_async_remote_copy(
+                src_ref=src,
+                dst_ref=dst,
+                send_sem=send_sem.at[SEM[name + "_near"]],
+                recv_sem=recv_sem.at[SEM[name]],
+                device_id=target,
+                device_id_type=MESH,
+            )
+            here_copy = pltpu.make_async_copy(src, dst, recv_sem.at[SEM[name]])
+            pl.when(jnp.logical_not(is_final))(near_copy.start)
+            pl.when(is_final)(here_copy.start)
+
+    near = [[video_over_audio(pair, h, 0) for h in range(GROUP)] for pair in pairs]
     arrived(squery.at[rows(32, 96)], "sqx")
     arrived(sblock.at[rows(128, 128)], "sib_s")
     results = [
@@ -458,59 +513,6 @@
         else:
             pack(spartials, dx, results, 32 * dx, 32 * dx + 16)
 
-    arrived(vk.at[rows(256, 256)], "sib_k")
-    arrived(vv.at[rows(256, 256)], "sib_v")
-    summed = [
-        [near_results[h] + audio_over_video(pair, h, 256) for h in range(GROUP)]
-        for pair, near_results in zip(pairs, near)
-    ]
-    for pair, results in zip(pairs, summed):
-        for n, dx in enumerate(pair):
-            for dy in (2, 1, 3, 0):
-                slot = 4 * dx + dy
-                row = 128 * n + 16 * dy
-                if slot:
-                    pack(partial, slot, results, row, row + 64)
-                    start(partial.at[slot], partials.at[slot], "rs", at(dx=-dx, dy=-dy))
-                else:
-                    pack(partials, slot, results, row, row + 64)
-
-    gathered(g1, "g1")
-    start(g1.at[rows(0, 512)], g1.at[rows(512, 512)], "sib_g", sibling)
-    arrived(vq.at[rows(64, 192)], "zq")
-
-    def video_over_audio(pair, h, first):
-        return weigh(
-            jnp.concatenate([vq[64 * d : 64 * d + 64, head(h)] for d in pair], axis=0),
-            g1[first : first + 512, head(h, CK)],
-            jnp.concatenate(
-                [g1[first : first + 512, head(h, CV)], g1[first : first + 512, KEEP:KV_LANES]],
-                axis=1,
-            ),
-        )
-
-    final_cfg = lax.rem(zh, 2)
-    is_final = cfg == final_cfg
-    slot_out = cfg * 2 + zh // 2
-
-    def final(src, dst, name, d):
-        target = device(final_cfg, x, plus(zh, -d), y, core)
-        if d:
-            start(src, dst, name, target)
-        else:
-            near_copy = pltpu.make_async_remote_copy(
-                src_ref=src,
-                dst_ref=dst,
-                send_sem=send_sem.at[SEM[name + "_near"]],
-                recv_sem=recv_sem.at[SEM[name]],
-                device_id=target,
-                device_id_type=MESH,
-            )
-            here_copy = pltpu.make_async_copy(src, dst, recv_sem.at[SEM[name]])
-            pl.when(jnp.logical_not(is_final))(near_copy.start)
-            pl.when(is_final)(here_copy.start)
-
-    near = [[video_over_audio(pair, h, 0) for h in range(GROUP)] for pair in pairs]
     arrived(g1.at[rows(512, 512)], "sib_g")
     summed = [
         [near_results[h] + video_over_audio(pair, h, 512) for h in range(GROUP)]
@@ -550,9 +552,9 @@
         sent(stage1.at[rows(0, 3)], name)
     for name in ("zk", "zv", "zq"):
         sent(vk.at[rows(0, 192)], name)
-    for name, ref in (("g0", g0), ("g1", g1)):
-        for kind, count in (("ax", 48), ("by", 48), ("ay", 192), ("bx", 192)):
-            sent(ref.at[rows(0, count)], name + kind)
+    sent(g0.at[rows(32, 480)], "g0")
+    for kind, count in (("ax", 48), ("by", 48), ("ay", 192), ("bx", 192)):
+        sent(g1.at[rows(0, count)], "g1" + kind)
     sent(squery.at[rows(0, 96)], "sqx")
     sent(sblock.at[rows(0, 96)], "sky")
     sent(vk.at[rows(0, 256)], "sib_k")

time: 44.6 us -> 43.8 us (0.982)
  Pallas kernels: 43.9 us -> 42.7 us
    pallas_call x1, Pallas kernels: 42.3 us -> 41.1 us  [per_device(): pl.pallas_call(kernel, out_shape=(jax.ShapeDtypeStruct((4, 64, GW), bf16)...]
where the time goes in v4:
time: 43.8 us; the launch traced here: 43.4 us
  Pallas kernels  42.7 us (97%)
  between operations  0.65 us (1%)
    pallas_call x1, Pallas kernels, per_device(): pl.pallas_call(kernel, out_shape=(jax.ShapeDtypeStruct((4, 64, GW), bf16)...  41.1 us
    pallas_call x1, Pallas kernels, per_device(): pl.pallas_call(guide_kernel, out_shape=(jax.ShapeDtypeStruct((64, 2 * GW)...  1.61 us

profile of v4, /device:TPU:1, one launch (start us, length us, event | category | flops | bytes accessed | tf_op | source)
XLA Modules:
  0.0 43.4 jit_solution(16777316326533658854)
XLA Ops:
  0.6 41.1 %shard_map.203 = (bf16[4,64,384]{2,1,0:T(8,128)(2,1)}, f32[4,8,384]{2,1,0:T(8,128)}) custom-call(bf16[1,64,3072]{2,1,0:T(8,128)(2,1)} %hidden_hbm.1, bf16[3072,1536]{1,0:T(8,128)(2,1)} %weight.1, bf16[1,64,1536]{2,1,0:T(8,128)(2,1)} %video_key_hbm.1, bf16[1,64,1536]{2,1,0:T(8,128)(2,1)} %video_value.1, bf16[1,8,1536]{2,1,0:T(8,128)(2,1)} %cross_key_hbm.1, ...), custom_call_target="tpu_custom_call" | custom-call | flops 1811939328 | bytes 12000000 | tf_op jit(solution)/shard_map/pallas_call | solution.py:622
  41.8 1.6 %shard_map.204 = (bf16[64,768]{1,0:T(8,128)(2,1)}, bf16[8,768]{1,0:T(8,128)(2,1)}) custom-call(bf16[4,64,384]{2,1,0:T(8,128)(2,1)} %get-tuple-element.4.video, f32[4,8,384]{2,1,0:T(8,128)} %get-tuple-element.5.audio), custom_call_target="tpu_custom_call" | custom-call | tf_op jit(solution)/shard_map/pallas_call | solution.py:691

commit v5 on v4

--- a/solution.py
+++ b/solution.py
@@ -173,11 +173,12 @@
 
     barrier = pltpu.get_barrier_semaphore()
     peers = [sibling]
-    for dx in range(4):
-        for dy in range(4):
-            if dx or dy:
-                peers.append(at(dx=dx, dy=dy))
-    for d in range(4):
+    for far in range(1, 5):
+        for dx in range(4):
+            for dy in range(4):
+                if min(dx, 4 - dx) + min(dy, 4 - dy) == far:
+                    peers.append(at(dx=dx, dy=dy))
+    for d in (0, 1, 3, 2):
         if d:
             peers.append(at(dz=d))
         peers.append(device(1 - cfg, x, plus(zh, d), y, core))
@@ -442,11 +443,10 @@
 
     arrived(vk.at[rows(256, 256)], "sib_k")
     arrived(vv.at[rows(256, 256)], "sib_v")
-    summed = [
-        [near_results[h] + audio_over_video(pair, h, 256) for h in range(GROUP)]
-        for pair, near_results in zip(pairs, near)
-    ]
-    for pair, results in zip(pairs, summed):
+    for pair, near_results in zip(pairs, near):
+        results = [
+            near_results[h] + audio_over_video(pair, h, 256) for h in range(GROUP)
+        ]
         for n, dx in enumerate(pair):
             for dy in (2, 1, 3, 0):
                 slot = 4 * dx + dy

time: 43.8 us -> 44.1 us (level)
  Pallas kernels: 42.7 us -> 43.4 us
    pallas_call x1, Pallas kernels: 41.1 us -> 41.7 us  [per_device(): pl.pallas_call(kernel, out_shape=(jax.ShapeDtypeStruct((4, 64, GW), bf16)...]
where the time goes in v5:
time: 44.1 us; the launch traced here: 44 us
  Pallas kernels  43.4 us (98%)
  between operations  0.65 us (1%)
    pallas_call x1, Pallas kernels, per_device(): pl.pallas_call(kernel, out_shape=(jax.ShapeDtypeStruct((4, 64, GW), bf16)...  41.7 us
    pallas_call x1, Pallas kernels, per_device(): pl.pallas_call(guide_kernel, out_shape=(jax.ShapeDtypeStruct((64, 2 * GW)...  1.61 us

profile of v5, /device:TPU:1, one launch (start us, length us, event | category | flops | bytes accessed | tf_op | source)
XLA Modules:
  0.0 44.0 jit_solution(13176909025246133002)
XLA Ops:
  0.6 41.7 %shard_map.203 = (bf16[4,64,384]{2,1,0:T(8,128)(2,1)}, f32[4,8,384]{2,1,0:T(8,128)}) custom-call(bf16[1,64,3072]{2,1,0:T(8,128)(2,1)} %hidden_hbm.1, bf16[3072,1536]{1,0:T(8,128)(2,1)} %weight.1, bf16[1,64,1536]{2,1,0:T(8,128)(2,1)} %video_key_hbm.1, bf16[1,64,1536]{2,1,0:T(8,128)(2,1)} %video_value.1, bf16[1,8,1536]{2,1,0:T(8,128)(2,1)} %cross_key_hbm.1, ...), custom_call_target="tpu_custom_call" | custom-call | flops 1811939328 | bytes 12000000 | tf_op jit(solution)/shard_map/pallas_call | solution.py:622
  42.4 1.6 %shard_map.204 = (bf16[64,768]{1,0:T(8,128)(2,1)}, bf16[8,768]{1,0:T(8,128)(2,1)}) custom-call(bf16[4,64,384]{2,1,0:T(8,128)(2,1)} %get-tuple-element.4.video, f32[4,8,384]{2,1,0:T(8,128)} %get-tuple-element.5.audio), custom_call_target="tpu_custom_call" | custom-call | tf_op jit(solution)/shard_map/pallas_call | solution.py:691
